TPU v7x, 512 devices: a whole 4x4x16 slice. The times are simulated.
512 devices in a mesh: group: 8 (over x_hi, y), ctx: 64 (over z, x_lo, core).
Axes of the slice: x: 4 (x_hi: 2, x_lo: 2; x = x_hi * 2 + x_lo), y: 4, z: 16, core: 2. Of those that a mesh axis runs over, the one named last changes fastest.
Arguments:
- queries: bfloat16 [11264, 2048], P('ctx', 'group'), may hold values from -30 to 30
- key_rows: bfloat16 [11264, 2048], P('ctx', 'group'), may hold values from -30 to 30
- value_rows: bfloat16 [11264, 2048], P('ctx', 'group'), may hold values from -6 to 6
- query_dir: bfloat16 [11264, 2048], P('ctx', 'group'), may hold values from -12 to 12
- out_weight: bfloat16 [2048, 3072], P('group'), may hold values from -0.125 to 0.125
Outputs:
- query_next: float32 [11264, 2048], P('ctx', 'group')
All inputs are finite; a program needn't handle non-finite values.
Results may differ from a plain program's by a relative error of at most 0.017.
Values may be sent and summed in bfloat16 or wider, within the bound.
A program may use at most 128 MiB of HBM per device.

v0:
```python
import math

import jax
import jax.numpy as jnp
from jax import lax
from jax.sharding import PartitionSpec as P

HEAD_DIM = 128


def heads_view(matrix):
    return matrix.reshape(matrix.shape[0], matrix.shape[1] // HEAD_DIM, HEAD_DIM)


def sweep_blocks(step_fn, initial, gathered, rows_here, shard_count):
    fitting = max(1, 1024 // rows_here)
    power_two = 1 << fitting.bit_length() - 1
    shards_each = math.gcd(shard_count, power_two)
    block_rows = rows_here * shards_each
    block_count = shard_count // shards_each

    def one_block(index, carry):
        start = index * block_rows
        pieces = tuple(
            (lax.dynamic_slice_in_dim(whole, start, block_rows, 0) for whole in gathered)
        )
        return step_fn(carry, pieces, start)

    return lax.fori_loop(0, block_count, one_block, initial)


def body(queries, key_rows, value_rows, query_dir, out_weight):
    scaling = HEAD_DIM ** (-0.5)
    own_queries = heads_view(queries)
    own_dir = heads_view(query_dir)
    rows_here = queries.shape[0]
    heads_here = queries.shape[1] // HEAD_DIM
    shard_count = lax.axis_size("ctx")
    dir_float = query_dir.astype(jnp.float32)
    residual_part = jnp.sum(dir_float * dir_float)
    residual_sq = lax.psum(residual_part, ("group", "ctx"))

    def add_keys(running, pieces, offset):
        highest, totals, weighted_sum, mixed_sum, tangent_mixed = running
        key_piece = heads_view(pieces[0])
        value_piece = heads_view(pieces[1])
        scores = (
            jnp.einsum("thd,shd->hts", own_queries, key_piece, preferred_element_type=jnp.float32)
            * scaling
        )
        tangent_scores = (
            jnp.einsum("thd,shd->hts", own_dir, key_piece, preferred_element_type=jnp.float32)
            * scaling
        )
        new_high = jnp.maximum(highest, jnp.max(scores, axis=2))
        factor = jnp.exp(highest - new_high)
        weights = jnp.exp(scores - new_high[:, :, None])
        weighted = weights * tangent_scores
        rounded = weights.astype(jnp.bfloat16)
        totals = totals * factor + jnp.sum(weights, axis=2)
        weighted_sum = weighted_sum * factor + jnp.sum(weighted, axis=2)
        mixed_sum = mixed_sum * factor[:, :, None] + jnp.einsum(
            "hts,shd->htd", rounded, value_piece, preferred_element_type=jnp.float32
        )
        tangent_mixed = tangent_mixed * factor[:, :, None] + jnp.einsum(
            "hts,shd->htd",
            weighted.astype(jnp.bfloat16),
            value_piece,
            preferred_element_type=jnp.float32,
        )
        return (new_high, totals, weighted_sum, mixed_sum, tangent_mixed)

    row_zeros = jnp.zeros((heads_here, rows_here), jnp.float32)
    block_zeros = jnp.zeros((heads_here, rows_here, HEAD_DIM), jnp.float32)
    initial = (
        jnp.full((heads_here, rows_here), -1e30, jnp.float32),
        row_zeros,
        row_zeros,
        block_zeros,
        block_zeros,
    )
    gathered = (
        lax.all_gather(key_rows, "ctx", axis=0, tiled=True),
        lax.all_gather(value_rows, "ctx", axis=0, tiled=True),
    )
    running = sweep_blocks(add_keys, initial, gathered, rows_here, shard_count)
    highest, totals, weighted_sum, mixed_sum, tangent_mixed = running
    attended = mixed_sum / totals[:, :, None]
    tangent = tangent_mixed / totals[:, :, None] - (weighted_sum / totals)[:, :, None] * attended
    log_total = highest + jnp.log(totals)
    tangent_rows = (
        tangent.astype(jnp.bfloat16).transpose(1, 0, 2).reshape(rows_here, heads_here * HEAD_DIM)
    )
    partial_proj = jnp.dot(tangent_rows, out_weight, preferred_element_type=jnp.float32)
    projected = lax.psum(partial_proj.astype(jnp.bfloat16), "group").astype(jnp.float32)
    col_width = projected.shape[1] // lax.axis_size("group")
    own_columns = lax.dynamic_slice_in_dim(
        projected, lax.axis_index("group") * col_width, col_width, 1
    )
    curve_part = jnp.sum(own_columns * own_columns)
    projected_low = projected.astype(jnp.bfloat16)
    curvature = lax.psum(curve_part, ("group", "ctx"))
    cotangent = lax.dot_general(
        projected_low, out_weight, (((1,), (1,)), ((), ())), preferred_element_type=jnp.float32
    ).astype(jnp.bfloat16)
    cotangent_heads = heads_view(cotangent)
    centering = jnp.sum(cotangent_heads.astype(jnp.float32) * attended.transpose(1, 0, 2), axis=2).T

    def add_back(query_grad, pieces, offset):
        key_piece = heads_view(pieces[0])
        value_piece = heads_view(pieces[1])
        scores = (
            jnp.einsum("thd,shd->hts", own_queries, key_piece, preferred_element_type=jnp.float32)
            * scaling
        )
        probabilities = jnp.exp(scores - log_total[:, :, None])
        back_scores = jnp.einsum(
            "thd,shd->hts", cotangent_heads, value_piece, preferred_element_type=jnp.float32
        )
        score_grad = probabilities * (back_scores - centering[:, :, None])
        return (
            query_grad
            + jnp.einsum(
                "hts,shd->htd",
                score_grad.astype(jnp.bfloat16),
                key_piece,
                preferred_element_type=jnp.float32,
            )
            * scaling
        )

    query_grad = sweep_blocks(add_back, block_zeros, gathered, rows_here, shard_count)
    step_size = residual_sq / curvature
    return dir_float - step_size * query_grad.transpose(1, 0, 2).reshape(
        rows_here, heads_here * HEAD_DIM
    )


def solution(mesh):
    in_specs = (
        P("ctx", "group"),
        P("ctx", "group"),
        P("ctx", "group"),
        P("ctx", "group"),
        P("group", None),
    )
    out_specs = P("ctx", "group")
    return jax.shard_map(body, mesh=mesh, in_specs=in_specs, out_specs=out_specs, check_vma=False)
```

profile of v0, /device:TPU:1, one launch (start us, length us, event | category | flops | bytes accessed | tf_op | source)
XLA Modules:
  0.0 635.1 jit_solution(6297663476645351550)
XLA Ops:
  9.1 132.7 %all-gather.3.cloned.1.call-done = bf16[11264,256]{1,0:T(8,128)(2,1)} async-done(((bf16[176,256]{1,0:T(8,128)(2,1)}), bf16[11264,256]{1,0:T(8,128)(2,1)}) %all-gather.3.cloned.1.call-update) | async-done | bytes 5767184 | tf_op jit(solution)/shard_map/all_gather | solution.py:83
  141.7 125.0 %all-gather.5.cloned.1.call-done = bf16[11264,256]{1,0:T(8,128)(2,1)} async-done(((bf16[176,256]{1,0:T(8,128)(2,1)}), bf16[11264,256]{1,0:T(8,128)(2,1)}) %all-gather.5.cloned.1.call-update) | async-done | bytes 5767184 | tf_op jit(solution)/shard_map/all_gather | solution.py:84
  266.7 90.6 %while.36 = (s32[]{:T(128)}, f32[2,176]{1,0:T(2,128)}, f32[2,176]{1,0:T(2,128)}, f32[2,176]{1,0:T(2,128)}, f32[2,176,128]{2,1,0:T(8,128)}, /*index=5*/f32[2,176,...) while((s32[]{:T(128)}, f32[2,176]{1,0:T(2,128)}, ...), condition=%wide.region_6.0_spmd.clone, body=%wide.region_2.0_spmd.clone.sunk | while | flops 256754080 | bytes 11685441 | solution.py:29
  272.4 1.2 dynamic-slice_bitcast_fusion.6
  278.0 1.2 dynamic-slice_bitcast_fusion.6
  283.7 1.2 dynamic-slice_bitcast_fusion.6
  295.0 1.2 dynamic-slice_bitcast_fusion.6
  306.4 1.2 dynamic-slice_bitcast_fusion.6
  312.0 1.2 dynamic-slice_bitcast_fusion.6
  317.7 1.2 dynamic-slice_bitcast_fusion.6
  323.4 1.2 dynamic-slice_bitcast_fusion.6
  334.7 1.2 dynamic-slice_bitcast_fusion.6
  346.0 1.2 dynamic-slice_bitcast_fusion.6
  351.7 1.2 dynamic-slice_bitcast_fusion.6
  357.4 1.3 fusion.43
  358.7 2.6 convolution_convert_fusion
  362.8 93.2 %all-reduce.3.cloned.1.call-done = bf16[176,3072]{1,0:T(8,128)(2,1)} async-done(((bf16[176,3072]{1,0:T(8,128)(2,1)}), bf16[176,3072]{1,0:T(8,128)(2,1)}) %all-reduce.3.cloned.1.call-update) | async-done | bytes 1081360 | tf_op jit(solution)/shard_map/psum | solution.py:95
  456.0 1.9 fusion.35
  459.0 1.6 multiply_reduce_fusion
  460.6 58.1 %while.37 = (s32[]{:T(128)}, f32[2,176,128]{2,1,0:T(8,128)}, bf16[11264,256]{1,0:T(8,128)(2,1)}, bf16[176,2,128]{2,0,1:T(8,128)(2,1)S(1)}, f32[2,176]{1,0:T(2,12...) while((s32[]{:T(128)}, f32[2,176,128]{2,1,0:T(8,128)}, ...), condition=%wide.region_12.0_spmd.clone, body=%wide.region_11.0_spmd.clone.sunk | while | flops 191690752 | bytes 5054925 | solution.py:29
  462.1 1.8 fusion.93
  465.5 2.1 fusion.93
  467.6 1.2 dynamic-slice_bitcast_fusion.7
  469.2 2.1 fusion.93
  471.2 1.2 dynamic-slice_bitcast_fusion.7
  472.8 2.1 fusion.93
  474.9 1.2 dynamic-slice_bitcast_fusion.7
  476.5 2.1 fusion.93
  478.5 1.2 dynamic-slice_bitcast_fusion.7
  480.1 2.1 fusion.93
  483.7 2.1 fusion.93
  485.8 1.2 dynamic-slice_bitcast_fusion.7
  487.4 2.1 fusion.93
  489.5 1.2 dynamic-slice_bitcast_fusion.7
  491.0 2.1 fusion.93
  493.1 1.2 dynamic-slice_bitcast_fusion.7
  494.7 2.1 fusion.93
  496.8 1.2 dynamic-slice_bitcast_fusion.7
  498.3 2.1 fusion.93
  502.0 2.1 fusion.93
  504.1 1.2 dynamic-slice_bitcast_fusion.7
  505.6 2.1 fusion.93
  507.7 1.2 dynamic-slice_bitcast_fusion.7
  509.3 2.1 fusion.93
  512.9 2.1 fusion.93
  516.6 2.1 fusion.93
  518.6 107.1 %all-reduce = (f32[]{:T(128)}, f32[]{:T(128)}) all-reduce(f32[]{:T(128)} %fusion.36, f32[]{:T(128)} %multiply_reduce_fusion), channel_id=1, replica_groups=mesh['group'=8,'ctx'=64] {'group','ctx'}, use_global_device_ids=true, to_apply=%region_1.0 | all-reduce | flops 2 | bytes 16 | tf_op jit(solution)/shard_map/psum | solution.py:41
  627.0 1.7 convert_subtract_fusion
  (517 shorter events, 93.1 us)
Async XLA Ops:
  6.5 352.1 %copy-start = (bf16[256,3072]{1,0:T(8,128)(2,1)S(1)}, bf16[256,3072]{1,0:T(8,128)(2,1)}, u32[]{:S(2)}) copy-start(bf16[256,3072]{1,0:T(8,128)(2,1)} %param.13) | copy-start | bytes 4718596
  6.5 135.2 %all-gather.3.cloned.1.call-start = ((), (), s32[]{:S(2)}) async-start(), calls=%async_computation | async-start | bytes 5857280 | tf_op jit(solution)/shard_map/all_gather | solution.py:83
  7.3 259.5 %all-gather.5.cloned.1.call-start = ((), (), s32[]{:S(2)}) async-start(), calls=%async_computation.1 | async-start | bytes 5857280 | tf_op jit(solution)/shard_map/all_gather | solution.py:84
  8.0 448.0 %all-reduce.3.cloned.1.call-start = ((), (), s32[]{:S(2)}) async-start(), calls=%async_computation.2 | async-start | bytes 2162688 | tf_op jit(solution)/shard_map/psum | solution.py:95
  270.1 1.3 copy-start.13
  270.4 1.3 copy-start.7
  274.5 1.2 copy-start.6
  275.8 1.3 copy-start.13
  276.1 1.3 copy-start.7
  280.2 1.2 copy-start.6
  281.4 1.3 copy-start.13
  281.8 1.3 copy-start.7
  285.9 1.2 copy-start.6
  287.1 1.3 copy-start.13
  287.4 1.3 copy-start.7
  291.5 1.2 copy-start.6
  292.8 1.3 copy-start.13
  293.1 1.3 copy-start.7
  297.2 1.2 copy-start.6
  298.4 1.3 copy-start.13
  298.8 1.3 copy-start.7
  302.9 1.2 copy-start.6
  304.1 1.3 copy-start.13
  304.4 1.3 copy-start.7
  309.8 1.3 copy-start.13
  310.1 1.3 copy-start.7
  314.2 1.2 copy-start.6
  315.4 1.3 copy-start.13
  315.8 1.3 copy-start.7
  319.9 1.2 copy-start.6
  321.1 1.3 copy-start.13
  321.4 1.3 copy-start.7
  325.5 1.2 copy-start.6
  326.8 1.3 copy-start.13
  327.1 1.3 copy-start.7
  331.2 1.2 copy-start.6
  332.4 1.3 copy-start.13
  332.8 1.3 copy-start.7
  338.1 1.3 copy-start.13
  338.4 1.3 copy-start.7
  343.8 1.3 copy-start.13
  344.1 1.3 copy-start.7
  349.4 1.3 copy-start.13
  349.8 1.3 copy-start.7
  355.1 1.3 copy-start.13
  355.4 1.3 copy-start.7
  362.8 95.1 %copy-start.3 = (f32[2,176,128]{2,1,0:T(8,128)S(1)}, f32[2,176,128]{2,1,0:T(8,128)}, u32[]{:S(2)}) copy-start(f32[2,176,128]{2,1,0:T(8,128)} %get-tuple-element.320) | copy-start | bytes 540676
  362.8 95.1 %copy-start.10 = (f32[2,176]{1,0:T(2,128)S(1)}, f32[2,176]{1,0:T(2,128)}, u32[]{:S(2)}) copy-start(f32[2,176]{1,0:T(2,128)} %get-tuple-element.318) | copy-start | bytes 4228
  (119 other events, 118.2 us)
Sparse Core Ops, SparseCore 0:
  9.5 132.1 all-gather.2
  143.9 122.7 all-gather.4
  361.4 94.5 all-reduce.2
where the time goes:
time: 637 us; the launch traced here: 635 us
  waiting for transfers between devices  352 us (55%)
  blocking collectives  107 us (17%)
  matrix products  76.7 us (12%)
  local copies, waits for them, and re-layouts  59.6 us (9%)
  other arithmetic  22.9 us (4%)
  between operations  14.5 us (2%)
    all_gather x1, waiting for transfers between devices, body(): lax.all_gather(key_rows, 'ctx', axis=0, tiled=True)  133 us
    all_gather x1, waiting for transfers between devices, body(): lax.all_gather(value_rows, 'ctx', axis=0, tiled=True)  125 us
    psum x1, blocking collectives, body(): residual_sq = lax.psum(residual_part, ('group', 'ctx'))  107 us
    psum x1, waiting for transfers between devices, body(): lax.psum(partial_proj.astype(jnp.bfloat16), 'group').astype(jnp.float32)  93.2 us
    while x368, local copies, waits for them, and re-layouts  57 us
    dot_general x16, matrix products, add_back(): jnp.einsum('hts,shd->htd', score_grad.astype(jnp.bfloat16), key_piece, pr...  33 us
    dot_general x16, matrix products, add_keys(): jnp.einsum('thd,shd->hts', own_queries, key_piece, preferred_element_type...  15.3 us
  transfers between devices with their start and end apart: 3, of which 3 were waited for; matrix products, arithmetic and copies ran while one was open for 0% of the time, Pallas kernels for 0%

commit v1 on v0

v1 whole, which is shorter than its diff:
```python
import functools
import math

import jax
import jax.numpy as jnp
from jax import lax
from jax.experimental import pallas as pl
from jax.experimental.pallas import tpu as pltpu
from jax.sharding import PartitionSpec as P

MESH = pl.DeviceIdType.MESH
HEAD_DIM = 128
SCALING = HEAD_DIM ** (-0.5)
EXP2_SCALE = SCALING * math.log2(math.e)
N_Y, N_XLO, N_CORE = 4, 2, 2
WINDOW = 48
F32, BF16 = jnp.float32, jnp.bfloat16


def dot_nt(a, b):
    return lax.dot_general(a, b, (((1,), (1,)), ((), ())), preferred_element_type=F32)


def dot_nn(a, b):
    return lax.dot_general(a, b, (((1,), (0,)), ((), ())), preferred_element_type=F32)


def kernel(
    n_group, n_z, rows,
    q_ref, k_ref, v_ref, d_ref, w_ref, out_ref,
    kv, qd, pw, highs, high, acc, dirb, att, tbuf, tin, wbuf, plow, cout, cin, cbuf, qg, qg_in,
    red_z, red_g, red_c,
    local_sem, swap_send, swap_recv, ring_send, ring_recv, sib_send, sib_recv,
    w_send, w_recv, t_send, t_recv, c_send, c_recv, red_send, red_recv, back_send, back_recv,
):
    group, ctx = lax.axis_index("group"), lax.axis_index("ctx")
    x_hi, y = lax.div(group, N_Y), lax.rem(group, N_Y)
    z, x_lo, core = lax.div(ctx, 4), lax.rem(lax.div(ctx, 2), 2), lax.rem(ctx, 2)
    head = 2 * group + x_lo
    both = 2 * rows
    unit = 4 * rows
    half_z = n_z // 2
    n_heads = 2 * n_group
    wide = wbuf.shape[1]

    def at_ctx(z_, x_lo_, core_):
        return 4 * z_ + 2 * x_lo_ + core_

    z_next, z_prev = lax.rem(z + 1, n_z), lax.rem(z + n_z - 1, n_z)
    dev_next = (group, at_ctx(z_next, x_lo, core))
    dev_prev = (group, at_ctx(z_prev, x_lo, core))
    dev_sib = (group, at_ctx(z, x_lo, 1 - core))
    dev_pair = (group, at_ctx(z, 1 - x_lo, core))
    dev_across = ((1 - x_hi) * N_Y + y, at_ctx(z, 1 - x_lo, core))
    y_next, y_prev = lax.rem(y + 1, N_Y), lax.rem(y + N_Y - 1, N_Y)
    dev_up = (x_hi * N_Y + y_next, ctx)
    dev_down = (x_hi * N_Y + y_prev, ctx)

    def remote(src, dst, send, recv, device):
        return pltpu.make_async_remote_copy(
            src_ref=src, dst_ref=dst, send_sem=send, recv_sem=recv,
            device_id=device, device_id_type=MESH,
        )

    def part_of(o):
        return x_lo + o - 2 * x_lo * o

    def chunk_rows(p, core_, j):
        start = lax.div(p, 2) * (2 * unit) + j * unit + lax.rem(p, 2) * both + core_ * rows
        return pl.ds(pl.multiple_of(start, 16), rows)

    def chunk(p, core_, j):
        return kv.at[chunk_rows(p, core_, j)]

    own_cols = pl.ds(pl.multiple_of(x_lo * HEAD_DIM, HEAD_DIM), HEAD_DIM)
    other_cols = pl.ds(pl.multiple_of((1 - x_lo) * HEAD_DIM, HEAD_DIM), HEAD_DIM)
    own_rows = pl.ds(pl.multiple_of(x_lo * rows, 16), rows)
    other_rows = pl.ds(pl.multiple_of((1 - x_lo) * rows, 16), rows)
    own_tan = pl.ds(pl.multiple_of(both + x_lo * rows, 16), rows)
    other_tan = pl.ds(pl.multiple_of(both + (1 - x_lo) * rows, 16), rows)
    first = chunk_rows(0, core, x_lo)
    second = chunk_rows(0, core, 1 - x_lo)
    own_half = pl.ds(pl.multiple_of(x_lo * wide, 128), wide)
    other_half = pl.ds(pl.multiple_of((1 - x_lo) * wide, 128), wide)

    def w_rows(x_hi_, y_, piece):
        start = (x_hi_ * N_Y + y_) * 256 + piece * 128
        return pl.ds(pl.multiple_of(start, 128), 128)

    local = [
        pltpu.make_async_copy(k_ref.at[:, own_cols], kv.at[first, 0:HEAD_DIM], local_sem.at[0]),
        pltpu.make_async_copy(
            v_ref.at[:, own_cols], kv.at[first, HEAD_DIM : 2 * HEAD_DIM], local_sem.at[1]
        ),
        pltpu.make_async_copy(q_ref.at[:, own_cols], qd.at[own_rows], local_sem.at[2]),
        pltpu.make_async_copy(d_ref.at[:, own_cols], qd.at[own_tan], local_sem.at[3]),
        pltpu.make_async_copy(d_ref, dirb, local_sem.at[4]),
        pltpu.make_async_copy(
            w_ref.at[:, own_half],
            wbuf.at[pl.ds(pl.multiple_of(group * 256, 256), 256)],
            local_sem.at[5],
        ),
    ]
    for copy in local:
        copy.start()

    barrier = pltpu.get_barrier_semaphore()

    def greet(device):
        pl.semaphore_signal(barrier, inc=1, device_id=device, device_id_type=MESH)

    @pl.loop(1, n_z)
    def _(i):
        greet((group, at_ctx(lax.rem(z + i, n_z), x_lo, core)))

    @pl.loop(1, n_group)
    def _(i):
        other = lax.rem(group + i, n_group)
        greet((other, at_ctx(z, x_lo, core)))
        greet((other, at_ctx(z, 1 - x_lo, core)))

    greet(dev_pair)
    greet(dev_sib)
    greet((group, at_ctx(z, 1 - x_lo, 1 - core)))
    pl.semaphore_wait(barrier, n_z - 1 + 2 * (n_group - 1) + 3)

    swap = [
        remote(
            k_ref.at[:, other_cols], kv.at[first, 0:HEAD_DIM],
            swap_send.at[0], swap_recv.at[0], dev_pair,
        ),
        remote(
            v_ref.at[:, other_cols], kv.at[first, HEAD_DIM : 2 * HEAD_DIM],
            swap_send.at[1], swap_recv.at[1], dev_pair,
        ),
        remote(
            q_ref.at[:, other_cols], qd.at[own_rows], swap_send.at[2], swap_recv.at[2], dev_pair
        ),
        remote(
            d_ref.at[:, other_cols], qd.at[own_tan], swap_send.at[3], swap_recv.at[3], dev_pair
        ),
    ]
    swap_in = [
        remote(
            k_ref.at[:, other_cols], kv.at[second, 0:HEAD_DIM],
            swap_send.at[0], swap_recv.at[0], dev_pair,
        ),
        remote(
            v_ref.at[:, other_cols], kv.at[second, HEAD_DIM : 2 * HEAD_DIM],
            swap_send.at[1], swap_recv.at[1], dev_pair,
        ),
        remote(
            q_ref.at[:, other_cols], qd.at[other_rows], swap_send.at[2], swap_recv.at[2], dev_pair
        ),
        remote(
            d_ref.at[:, other_cols], qd.at[other_tan], swap_send.at[3], swap_recv.at[3], dev_pair
        ),
    ]
    for copy in swap:
        copy.start()

    def ring(way, s, o, src_p, dst_p):
        j = part_of(o)
        return remote(
            chunk(src_p, core, j), chunk(dst_p, core, j),
            ring_send.at[way, s - 1, o], ring_recv.at[way, s - 1, o],
            dev_next if way == 0 else dev_prev,
        )

    def sibling(p, o, core_):
        place = chunk(p, core_, part_of(o))
        return remote(place, place, sib_send.at[p, o], sib_recv.at[p, o], dev_sib)

    local[0].wait()
    local[1].wait()
    ring(0, 1, 0, 0, 1).start()
    ring(1, 1, 0, 0, 2).start()
    sibling(0, 0, core).start()

    def w_copy(n, src, dst, device):
        return remote(src, dst, w_send.at[n], w_recv.at[n], device)

    def w_piece(x_hi_, y_, piece):
        return wbuf.at[w_rows(x_hi_, y_, piece)]

    def w_half(x_hi_, y_, part):
        start = (x_hi_ * N_Y + y_) * 256 + core * 128 + part * 64
        return wbuf.at[pl.ds(pl.multiple_of(start, 64), 64)]

    own_w = w_piece(x_hi, y, core)
    across_w = w_piece(1 - x_hi, y, core)
    y_far = lax.rem(y + 2, N_Y)
    w_src = w_ref.at[pl.ds(pl.multiple_of(core * 128, 128), 128), other_half]
    local[5].wait()
    w_copy(0, w_src, own_w, dev_across).start()
    w_copy(1, own_w, own_w, dev_up).start()
    w_copy(2, own_w, own_w, dev_down).start()

    swap_in[0].wait_recv()
    swap_in[1].wait_recv()
    ring(0, 1, 1, 0, 1).start()
    ring(1, 1, 1, 0, 2).start()
    sibling(0, 1, core).start()

    def w_sibling(n, x_hi_, y_, core_):
        place = w_piece(x_hi_, y_, core_)
        return w_copy(n, place, place, dev_sib)

    def w_middle():
        w_copy(0, across_w, across_w, dev_across).wait_recv()
        w_copy(5, across_w, across_w, dev_up).start()
        w_copy(6, across_w, across_w, dev_down).start()
        below, above = w_piece(x_hi, y_prev, core), w_piece(x_hi, y_next, core)
        w_copy(1, below, below, dev_up).wait_recv()
        onward = w_half(x_hi, y_prev, 0)
        w_copy(3, onward, onward, dev_up).start()
        w_copy(2, above, above, dev_down).wait_recv()
        onward = w_half(x_hi, y_next, 1)
        w_copy(4, onward, onward, dev_down).start()
        w_sibling(9, 1 - x_hi, y, core).start()
        w_sibling(10, x_hi, y_prev, core).start()
        w_sibling(11, x_hi, y_next, core).start()

    def w_late():
        below, above = w_piece(1 - x_hi, y_prev, core), w_piece(1 - x_hi, y_next, core)
        w_copy(5, below, below, dev_up).wait_recv()
        onward = w_half(1 - x_hi, y_prev, 0)
        w_copy(7, onward, onward, dev_up).start()
        w_copy(6, above, above, dev_down).wait_recv()
        onward = w_half(1 - x_hi, y_next, 1)
        w_copy(8, onward, onward, dev_down).start()
        w_sibling(13, 1 - x_hi, y_prev, core).start()
        w_sibling(14, 1 - x_hi, y_next, core).start()
        place = w_half(x_hi, y_far, 0)
        w_copy(3, place, place, dev_up).wait_recv()
        place = w_half(x_hi, y_far, 1)
        w_copy(4, place, place, dev_down).wait_recv()
        w_sibling(12, x_hi, y_far, core).start()

    def w_last():
        place = w_half(1 - x_hi, y_far, 0)
        w_copy(7, place, place, dev_up).wait_recv()
        place = w_half(1 - x_hi, y_far, 1)
        w_copy(8, place, place, dev_down).wait_recv()
        w_sibling(15, 1 - x_hi, y_far, core).start()

    def w_finish():
        w_sibling(9, 1 - x_hi, y, 1 - core).wait_recv()
        w_sibling(10, x_hi, y_prev, 1 - core).wait_recv()
        w_sibling(11, x_hi, y_next, 1 - core).wait_recv()
        w_sibling(12, x_hi, y_far, 1 - core).wait_recv()
        w_sibling(13, 1 - x_hi, y_prev, 1 - core).wait_recv()
        w_sibling(14, 1 - x_hi, y_next, 1 - core).wait_recv()
        w_sibling(15, 1 - x_hi, y_far, 1 - core).wait_recv()

    high[...] = jnp.full(high.shape, -1e30, F32)
    acc[...] = jnp.zeros(acc.shape, F32)
    for copy in local[2:5]:
        copy.wait()
    swap_in[2].wait_recv()
    swap_in[3].wait_recv()
    direction = dirb[...].astype(F32)
    squares = jnp.sum((direction * direction).reshape(rows // 8, 8, 2 * HEAD_DIM), axis=0)
    residual_part = squares[:, :HEAD_DIM] + squares[:, HEAD_DIM:]

    def service(h):
        b, o = lax.div(h, 2), lax.rem(h, 2)
        s = b + 1
        back_p, ahead_p = 2 * s - 1, 2 * s

        @pl.when(s < half_z)
        def _():
            ring(0, s, o, back_p, back_p).wait_recv()

            @pl.when(s + 1 < half_z)
            def _():
                ring(0, s + 1, o, back_p, back_p + 2).start()

            @pl.when((s + 1 == half_z) & (o == 0))
            def _():
                ring(0, s + 1, o, back_p, back_p + 2).start()

            ring(1, s, o, ahead_p, ahead_p).wait_recv()

            @pl.when(s + 1 < half_z)
            def _():
                ring(1, s + 1, o, ahead_p, ahead_p + 2).start()

            @pl.when((s + 1 == half_z) & (o == 1))
            def _():
                ring(1, s + 1, o, ahead_p, n_z - 1).start()

            sibling(back_p, o, core).start()
            sibling(ahead_p, o, core).start()

        @pl.when((s == half_z) & (o == 0))
        def _():
            ring(0, s, o, back_p, back_p).wait_recv()
            sibling(back_p, o, core).start()

        @pl.when((s == half_z) & (o == 1))
        def _():
            ring(1, s, o, back_p, back_p).wait_recv()
            sibling(back_p, o, core).start()

    def unit_rows(h):
        start = lax.div(h, 2) * (2 * unit) + part_of(lax.rem(h, 2)) * unit
        return pl.ds(pl.multiple_of(start, 16), unit)

    ones = jnp.ones((unit, HEAD_DIM), BF16)

    def forward(h):
        b, o = lax.div(h, 2), lax.rem(h, 2)

        @pl.when(b == 0)
        def _():
            sibling(0, o, 1 - core).wait_recv()

        sibling(2 * b + 1, o, 1 - core).wait_recv()

        @pl.when(b + 1 < half_z)
        def _():
            sibling(2 * b + 2, o, 1 - core).wait_recv()

        here = unit_rows(h)
        keys = kv[here, 0:HEAD_DIM]
        values = kv[here, HEAD_DIM : 2 * HEAD_DIM]
        scores = dot_nt(qd[0:both], keys)
        tangents = dot_nt(qd[both : 2 * both], keys)
        old = high[...]
        new = jnp.maximum(old, jnp.max(scores, axis=1, keepdims=True))
        high[...] = new
        highs[h] = new
        factor = jnp.exp2((old - new) * EXP2_SCALE)
        weights = jnp.exp2((scores - new) * EXP2_SCALE)
        weighted = weights * tangents
        pw[h, 0:both] = weights.astype(BF16)
        pw[h, both : 2 * both] = weighted.astype(BF16)
        mixed = dot_nn(pw[h], jnp.concatenate([values, ones], axis=1))
        acc[0:both] = acc[0:both] * factor + mixed[0:both]
        acc[both : 2 * both] = acc[both : 2 * both] * factor + mixed[both : 2 * both]

    n_units = n_z
    service(0)

    @pl.loop(1, n_units)
    def _(h):
        service(h)

        @pl.when(h == 5)
        def _():
            w_middle()

        @pl.when(h == 12)
        def _():
            w_late()

        forward(h - 1)

    w_last()
    forward(n_units - 1)

    totals = acc[0:both, HEAD_DIM : 2 * HEAD_DIM]
    attended = acc[0:both, 0:HEAD_DIM] / totals
    att[...] = attended
    tbuf[...] = (
        (acc[both : 2 * both, 0:HEAD_DIM] - acc[both : 2 * both, HEAD_DIM : 2 * HEAD_DIM] * attended)
        * (SCALING / totals)
    ).astype(BF16)

    def window_start(i):
        return lax.div(((both // 16 - 3) * i + 3), n_group - 1) * 16

    def window(i):
        return pl.ds(pl.multiple_of(window_start(i), 16), WINDOW)

    def head_cols(h_):
        return pl.ds(pl.multiple_of(h_ * HEAD_DIM, HEAD_DIM), HEAD_DIM)

    def t_copy(group_, x_lo_, slot):
        return remote(
            tbuf.at[window(group_)], tin.at[:, head_cols(head)],
            t_send.at[slot], t_recv.at[head], (group_, at_ctx(z, x_lo_, core)),
        )

    def t_arrival(h_):
        return remote(
            tbuf.at[window(0)], tin.at[:, head_cols(h_)], t_send.at[0], t_recv.at[h_], dev_pair
        )

    t_copy(group, 1 - x_lo, 0).start()

    @pl.loop(1, n_group)
    def _(i):
        other = lax.rem(group + i, n_group)
        t_copy(other, x_lo, 2 * i).start()
        t_copy(other, 1 - x_lo, 2 * i + 1).start()

    tin[:, head_cols(head)] = tbuf[window(group)]
    w_finish()

    @pl.loop(0, n_heads)
    def _(h_):
        @pl.when(h_ != head)
        def _():
            t_arrival(h_).wait_recv()

    counted = window_start(group + 1) - window_start(group)
    row_id = lax.broadcasted_iota(jnp.int32, (WINDOW, HEAD_DIM), 0)
    curve = jnp.zeros((8, HEAD_DIM), F32)
    step = wide // 3
    for n in range(3):
        cols = slice(n * step, (n + 1) * step)
        proj = dot_nn(tin[...], wbuf[:, cols])
        plow[:, cols] = proj.astype(BF16)
        squared = proj * proj
        lanes = squared[:, 0:HEAD_DIM]
        for m in range(1, step // HEAD_DIM):
            lanes = lanes + squared[:, m * HEAD_DIM : (m + 1) * HEAD_DIM]
        lanes = jnp.where(row_id < counted, lanes, 0.0)
        curve = curve + jnp.sum(lanes.reshape(WINDOW // 8, 8, HEAD_DIM), axis=0)

    def c_copy(h_):
        return remote(
            cout.at[:, head_cols(h_)], cin.at[x_lo, group],
            c_send.at[h_], c_recv.at[x_lo * n_group + group],
            (lax.div(h_, 2), at_ctx(z, lax.rem(h_, 2), core)),
        )

    def c_arrival(x_lo_, group_):
        return remote(
            cout.at[:, head_cols(0)], cin.at[x_lo_, group_],
            c_send.at[0], c_recv.at[x_lo_ * n_group + group_], dev_pair,
        )

    block = 512
    for n in range(n_heads * HEAD_DIM // block):
        at = slice(n * block, (n + 1) * block)
        cout[:, at] = dot_nt(plow[...], wbuf[at]).astype(BF16)

        @pl.loop(n * (block // HEAD_DIM), (n + 1) * (block // HEAD_DIM))
        def _(h_):
            @pl.when(h_ != head)
            def _():
                c_copy(h_).start()

    cin[x_lo, group] = cout[:, head_cols(head)]

    red_z[z, 0:8] = curve
    red_z[z, 8:16] = residual_part

    @pl.loop(1, n_z)
    def _(i):
        other = lax.rem(z + i, n_z)
        remote(
            red_z.at[z], red_z.at[z], red_send.at[i], red_recv.at[z],
            (group, at_ctx(other, x_lo, core)),
        ).start()

    @pl.loop(0, 2 * n_group)
    def _(i):
        x_lo_, group_ = lax.div(i, n_group), lax.rem(i, n_group)

        @pl.when(i != x_lo * n_group + group)
        def _():
            c_arrival(x_lo_, group_).wait_recv()

    starts = [((both // 16 - 3) * i + 3) // (n_group - 1) * 16 for i in range(n_group)]
    for i in range(n_group):
        cbuf[starts[i] : starts[i] + WINDOW] = (
            cin[0, i].astype(F32) + cin[1, i].astype(F32)
        ).astype(BF16)
    centering = jnp.sum(cbuf[...].astype(F32) * att[...], axis=1, keepdims=True)

    qg[...] = jnp.zeros(qg.shape, F32)

    def backward(h):
        here = unit_rows(h)
        keys = kv[here, 0:HEAD_DIM]
        values = kv[here, HEAD_DIM : 2 * HEAD_DIM]
        back = dot_nt(cbuf[...], values)
        grad = (pw[h, 0:both].astype(F32) * (back - centering)).astype(BF16)
        factor = jnp.exp2((highs[h] - high[...]) * EXP2_SCALE)
        qg[...] += dot_nn(grad, keys) * factor

    @pl.loop(0, 6)
    def _(h):
        backward(h)

    def red_arrival(buf, i, base):
        return remote(buf.at[i], buf.at[i], red_send.at[0], red_recv.at[base + i], dev_pair)

    @pl.loop(1, n_z)
    def _(i):
        red_arrival(red_z, lax.rem(z + i, n_z), 0).wait_recv()

    red_g[group] = jnp.sum(red_z[...], axis=0)

    @pl.loop(1, n_group)
    def _(i):
        other = lax.rem(group + i, n_group)
        remote(
            red_g.at[group], red_g.at[group], red_send.at[n_z + i], red_recv.at[n_z + group],
            (other, ctx),
        ).start()

    @pl.loop(6, 11)
    def _(h):
        backward(h)

    @pl.loop(1, n_group)
    def _(i):
        red_arrival(red_g, lax.rem(group + i, n_group), n_z).wait_recv()

    place = 2 * x_lo + core
    red_c[place] = jnp.sum(red_g[...], axis=0)

    @pl.loop(1, 4)
    def _(i):
        other = lax.rem(place + i, 4)
        remote(
            red_c.at[place], red_c.at[place],
            red_send.at[n_z + n_group + i], red_recv.at[n_z + n_group + place],
            (group, 4 * z + other),
        ).start()

    @pl.loop(11, n_units)
    def _(h):
        backward(h)

    scale = SCALING / acc[0:both, HEAD_DIM : 2 * HEAD_DIM]
    qg[...] = qg[...] * scale
    back_copy = remote(
        qg.at[other_rows], qg_in, back_send.at[0], back_recv.at[0], dev_pair
    )
    back_copy.start()

    @pl.loop(1, 4)
    def _(i):
        red_arrival(red_c, lax.rem(place + i, 4), n_z + n_group).wait_recv()

    sums = jnp.sum(red_c[...], axis=0)
    curvature = jnp.sum(jnp.sum(sums[0:8], axis=0, keepdims=True), axis=1, keepdims=True)
    residual_sq = jnp.sum(jnp.sum(sums[8:16], axis=0, keepdims=True), axis=1, keepdims=True)
    step_size = residual_sq / curvature
    out_ref[:, own_cols] = dirb[:, own_cols].astype(F32) - step_size * qg[own_rows]
    back_copy.wait_recv()
    out_ref[:, other_cols] = dirb[:, other_cols].astype(F32) - step_size * qg_in[...]

    back_copy.wait_send()
    for copy in swap:
        copy.wait_send()

    @pl.loop(0, 2 * (half_z - 1))
    def _(i):
        s, o = lax.div(i, 2) + 1, lax.rem(i, 2)
        ring(0, s, o, 1, 1).wait_send()
        ring(1, s, o, 1, 1).wait_send()
        sibling(2 * s - 1, o, core).wait_send()
        sibling(2 * s, o, core).wait_send()

    ring(0, half_z, 0, 1, 1).wait_send()
    ring(1, half_z, 1, 1, 1).wait_send()
    for o in range(2):
        sibling(0, o, core).wait_send()
        sibling(n_z - 1, o, core).wait_send()
    for n in (0, 1, 2, 5, 6):
        w_copy(n, own_w, own_w, dev_up).wait_send()
    for n in (3, 4, 7, 8):
        w_copy(n, w_half(x_hi, y, 0), w_half(x_hi, y, 0), dev_up).wait_send()
    for n in range(9, 16):
        w_sibling(n, x_hi, y, core).wait_send()
    t_copy(group, 1 - x_lo, 0).wait_send()

    @pl.loop(2, n_heads)
    def _(i):
        t_copy(0, 0, i).wait_send()

    @pl.loop(0, n_heads)
    def _(h_):
        @pl.when(h_ != head)
        def _():
            c_copy(h_).wait_send()

    def red_sent(buf, n):
        remote(buf.at[0], buf.at[0], red_send.at[n], red_recv.at[0], dev_pair).wait_send()

    @pl.loop(1, n_z)
    def _(i):
        red_sent(red_z, i)

    @pl.loop(1, n_group)
    def _(i):
        red_sent(red_g, n_z + i)

    @pl.loop(1, 4)
    def _(i):
        red_sent(red_c, n_z + n_group + i)


def body(n_group, n_z, queries, key_rows, value_rows, query_dir, out_weight):
    rows = queries.shape[0]
    both, unit = 2 * rows, 4 * rows
    width = out_weight.shape[1]
    n_heads = 2 * n_group
    any_spec = pl.BlockSpec(memory_space=pl.ANY)
    dma = pltpu.SemaphoreType.DMA
    n_red = n_z + n_group + 4
    return pl.pallas_call(
        functools.partial(kernel, n_group, n_z, rows),
        out_shape=jax.ShapeDtypeStruct((rows, 2 * HEAD_DIM), F32),
        in_specs=[any_spec] * 5,
        out_specs=pl.BlockSpec(memory_space=pltpu.VMEM),
        scratch_shapes=[
            pltpu.VMEM((n_z * unit, 2 * HEAD_DIM), BF16),
            pltpu.VMEM((2 * both, HEAD_DIM), BF16),
            pltpu.VMEM((n_z, 2 * both, unit), BF16),
            pltpu.VMEM((n_z, both, 1), F32),
            pltpu.VMEM((both, 1), F32),
            pltpu.VMEM((2 * both, 2 * HEAD_DIM), F32),
            pltpu.VMEM((rows, 2 * HEAD_DIM), BF16),
            pltpu.VMEM((both, HEAD_DIM), F32),
            pltpu.VMEM((both, HEAD_DIM), BF16),
            pltpu.VMEM((WINDOW, n_heads * HEAD_DIM), BF16),
            pltpu.VMEM((n_heads * HEAD_DIM, width // 2), BF16),
            pltpu.VMEM((WINDOW, width // 2), BF16),
            pltpu.VMEM((WINDOW, n_heads * HEAD_DIM), BF16),
            pltpu.VMEM((2, n_group, WINDOW, HEAD_DIM), BF16),
            pltpu.VMEM((both, HEAD_DIM), BF16),
            pltpu.VMEM((both, HEAD_DIM), F32),
            pltpu.VMEM((rows, HEAD_DIM), F32),
            pltpu.VMEM((n_z, 16, HEAD_DIM), F32),
            pltpu.VMEM((n_group, 16, HEAD_DIM), F32),
            pltpu.VMEM((4, 16, HEAD_DIM), F32),
            dma((6,)),
            dma((4,)), dma((4,)),
            dma((2, n_z // 2, 2)), dma((2, n_z // 2, 2)),
            dma((n_z, 2)), dma((n_z, 2)),
            dma((16,)), dma((16,)),
            dma((n_heads,)), dma((n_heads,)),
            dma((n_heads,)), dma((n_heads,)),
            dma((n_red,)), dma((n_red,)),
            dma((1,)), dma((1,)),
        ],
        compiler_params=pltpu.CompilerParams(
            collective_id=0, has_side_effects=True, vmem_limit_bytes=60 * 1024 * 1024
        ),
        name="gauss_newton_layer",
    )(queries, key_rows, value_rows, query_dir, out_weight)


def solution(mesh):
    n_group, n_ctx = mesh.shape["group"], mesh.shape["ctx"]
    in_specs = (
        P("ctx", "group"),
        P("ctx", "group"),
        P("ctx", "group"),
        P("ctx", "group"),
        P("group", None),
    )
    return jax.shard_map(
        functools.partial(body, n_group, n_ctx // (N_XLO * N_CORE)),
        mesh=mesh, in_specs=in_specs, out_specs=P("ctx", "group"), check_vma=False,
    )
```

time: 637 us -> 91.7 us (0.14)
  waiting for transfers between devices: 352 us -> 0 us
  blocking collectives: 107 us -> 0 us
  Pallas kernels: 0 us -> 88.7 us
  matrix products: 76.7 us -> 0 us
  local copies, waits for them, and re-layouts: 59.6 us -> 1.61 us
  other arithmetic: 22.9 us -> 0 us
  between operations: 14.5 us -> 0.01 us
    all_gather x2 -> x0, waiting for transfers between devices: 258 us -> none  [the longest x1 133 us: body(): lax.all_gather(key_rows, 'ctx', axis=0, tiled=True)]
    psum x1 -> x0, blocking collectives: 107 us -> none  [body(): residual_sq = lax.psum(residual_part, ('group', 'ctx'))]
    psum x1 -> x0, waiting for transfers between devices: 93.2 us -> none  [body(): lax.psum(partial_proj.astype(jnp.bfloat16), 'group').astype(jnp.float32)]
    pallas_call x0 -> x1, Pallas kernels: none -> 88.7 us  [body(): pl.pallas_call(functools.partial(kernel, n_group, n_z, rows), out_shape=j...]
    dot_general x98 -> x0, matrix products: 76.7 us -> none  [the longest x16 33 us: add_back(): jnp.einsum('hts,shd->htd', score_grad.astype(jnp.bfloat16), key_piece, pr...]
    while x368 -> x0, local copies, waits for them, and re-layouts: 57 us -> none
    max x16 -> x0, other arithmetic: 11.1 us -> none  [add_keys(): new_high = jnp.maximum(highest, jnp.max(scores, axis=2))]
    reduce_sum x19 -> x0, other arithmetic: 8.31 us -> none  [the longest x16 5.81 us: add_keys(): totals = totals * factor + jnp.sum(weights, axis=2)]
  transfers between devices with their start and end apart: 3 -> 0, of which waited for: 3 -> 0; matrix products, arithmetic and copies ran while one was open for 0% -> 0% of each run, Pallas kernels for 0% -> 0%
where the time goes in v1:
time: 91.7 us; the launch traced here: 90.3 us
  Pallas kernels  88.7 us (97%)
  local copies, waits for them, and re-layouts  1.61 us (2%)
    pallas_call x1, Pallas kernels, body(): pl.pallas_call(functools.partial(kernel, n_group, n_z, rows), out_shape=j...  88.7 us

profile of v1, /device:TPU:1, one launch (start us, length us, event | category | flops | bytes accessed | tf_op | source)
XLA Modules:
  0.0 90.3 jit_solution(18255354107485246632)
XLA Ops:
  0.0 88.7 %gauss_newton_layer.1 = f32[176,256]{1,0:T(8,128)} custom-call(bf16[176,256]{1,0:T(8,128)(2,1)} %q_ref.1, bf16[176,256]{1,0:T(8,128)(2,1)} %k_ref.1, bf16[176,256]{1,0:T(8,128)(2,1)} %v_ref.1, bf16[176,256]{1,0:T(8,128)(2,1)} %d_ref.1, bf16[256,3072]{1,0:T(8,128)(2,1)} %w_ref.1), custom_call_target="tpu_custom_call" | custom-call | tf_op jit(solution)/shard_map/gauss_newton_layer/pallas_call | solution.py:609
  88.7 1.6 %copy.7 = f32[176,256]{1,0:T(8,128)} copy(f32[176,256]{1,0:T(8,128)} %gauss_newton_layer.1) | data formatting | bytes 360448

commit v2 on v1

--- a/solution.py
+++ b/solution.py
@@ -109,20 +109,15 @@
     def greet(device):
         pl.semaphore_signal(barrier, inc=1, device_id=device, device_id_type=MESH)
 
-    @pl.loop(1, n_z)
-    def _(i):
-        greet((group, at_ctx(lax.rem(z + i, n_z), x_lo, core)))
-
-    @pl.loop(1, n_group)
-    def _(i):
+    greet(dev_next)
+    greet(dev_prev)
+    greet(dev_sib)
+    greet(dev_pair)
+    for i in range(1, n_group):
         other = lax.rem(group + i, n_group)
         greet((other, at_ctx(z, x_lo, core)))
         greet((other, at_ctx(z, 1 - x_lo, core)))
-
-    greet(dev_pair)
-    greet(dev_sib)
-    greet((group, at_ctx(z, 1 - x_lo, 1 - core)))
-    pl.semaphore_wait(barrier, n_z - 1 + 2 * (n_group - 1) + 3)
+    pl.semaphore_wait(barrier, 4 + 2 * (n_group - 1))
 
     swap = [
         remote(
@@ -156,14 +151,15 @@
             d_ref.at[:, other_cols], qd.at[other_tan], swap_send.at[3], swap_recv.at[3], dev_pair
         ),
     ]
-    for copy in swap:
-        copy.start()
-
-    def ring(way, s, o, src_p, dst_p):
+    swap[0].start()
+    swap[1].start()
+
+    def ring(way, s, o, f, src_p, dst_p):
         j = part_of(o)
+        cols = slice(f * HEAD_DIM, (f + 1) * HEAD_DIM)
         return remote(
-            chunk(src_p, core, j), chunk(dst_p, core, j),
-            ring_send.at[way, s - 1, o], ring_recv.at[way, s - 1, o],
+            kv.at[chunk_rows(src_p, core, j), cols], kv.at[chunk_rows(dst_p, core, j), cols],
+            ring_send.at[way, s - 1, o, f], ring_recv.at[way, s - 1, o, f],
             dev_next if way == 0 else dev_prev,
         )
 
@@ -173,8 +169,11 @@
 
     local[0].wait()
     local[1].wait()
-    ring(0, 1, 0, 0, 1).start()
-    ring(1, 1, 0, 0, 2).start()
+    for f in range(2):
+        ring(0, 1, 0, f, 0, 1).start()
+        ring(1, 1, 0, f, 0, 2).start()
+    swap[2].start()
+    swap[3].start()
     sibling(0, 0, core).start()
 
     def w_copy(n, src, dst, device):
@@ -196,10 +195,10 @@
     w_copy(1, own_w, own_w, dev_up).start()
     w_copy(2, own_w, own_w, dev_down).start()
 
-    swap_in[0].wait_recv()
-    swap_in[1].wait_recv()
-    ring(0, 1, 1, 0, 1).start()
-    ring(1, 1, 1, 0, 2).start()
+    for f in range(2):
+        swap_in[f].wait_recv()
+        ring(0, 1, 1, f, 0, 1).start()
+        ring(1, 1, 1, f, 0, 2).start()
     sibling(0, 1, core).start()
 
     def w_sibling(n, x_hi_, y_, core_):
@@ -268,39 +267,46 @@
         s = b + 1
         back_p, ahead_p = 2 * s - 1, 2 * s
 
+        @pl.when(s + 1 < half_z)
+        def _():
+            for f in range(2):
+                ring(0, s, o, f, back_p, back_p).wait_recv()
+                ring(0, s + 1, o, f, back_p, back_p + 2).start()
+                ring(1, s, o, f, ahead_p, ahead_p).wait_recv()
+                ring(1, s + 1, o, f, ahead_p, ahead_p + 2).start()
+
+        @pl.when(s + 1 == half_z)
+        def _():
+            for f in range(2):
+                ring(0, s, o, f, back_p, back_p).wait_recv()
+
+                @pl.when(o == 0)
+                def _():
+                    ring(0, s + 1, o, f, back_p, back_p + 2).start()
+
+                ring(1, s, o, f, ahead_p, ahead_p).wait_recv()
+
+                @pl.when(o == 1)
+                def _():
+                    ring(1, s + 1, o, f, ahead_p, n_z - 1).start()
+
         @pl.when(s < half_z)
         def _():
-            ring(0, s, o, back_p, back_p).wait_recv()
-
-            @pl.when(s + 1 < half_z)
-            def _():
-                ring(0, s + 1, o, back_p, back_p + 2).start()
-
-            @pl.when((s + 1 == half_z) & (o == 0))
-            def _():
-                ring(0, s + 1, o, back_p, back_p + 2).start()
-
-            ring(1, s, o, ahead_p, ahead_p).wait_recv()
-
-            @pl.when(s + 1 < half_z)
-            def _():
-                ring(1, s + 1, o, ahead_p, ahead_p + 2).start()
-
-            @pl.when((s + 1 == half_z) & (o == 1))
-            def _():
-                ring(1, s + 1, o, ahead_p, n_z - 1).start()
-
             sibling(back_p, o, core).start()
             sibling(ahead_p, o, core).start()
 
-        @pl.when((s == half_z) & (o == 0))
-        def _():
-            ring(0, s, o, back_p, back_p).wait_recv()
-            sibling(back_p, o, core).start()
-
-        @pl.when((s == half_z) & (o == 1))
-        def _():
-            ring(1, s, o, back_p, back_p).wait_recv()
+        @pl.when(s == half_z)
+        def _():
+            for f in range(2):
+
+                @pl.when(o == 0)
+                def _():
+                    ring(0, s, o, f, back_p, back_p).wait_recv()
+
+                @pl.when(o == 1)
+                def _():
+                    ring(1, s, o, f, back_p, back_p).wait_recv()
+
             sibling(back_p, o, core).start()
 
     def unit_rows(h):
@@ -389,9 +395,7 @@
         )
 
     t_copy(group, 1 - x_lo, 0).start()
-
-    @pl.loop(1, n_group)
-    def _(i):
+    for i in range(1, n_group):
         other = lax.rem(group + i, n_group)
         t_copy(other, x_lo, 2 * i).start()
         t_copy(other, 1 - x_lo, 2 * i + 1).start()
@@ -399,11 +403,33 @@
     tin[:, head_cols(head)] = tbuf[window(group)]
     w_finish()
 
-    @pl.loop(0, n_heads)
-    def _(h_):
-        @pl.when(h_ != head)
-        def _():
-            t_arrival(h_).wait_recv()
+    for copy in swap:
+        copy.wait_send()
+
+    @pl.loop(0, 2 * (half_z - 1))
+    def _(i):
+        s, o = lax.div(i, 2) + 1, lax.rem(i, 2)
+        for f in range(2):
+            ring(0, s, o, f, 1, 1).wait_send()
+            ring(1, s, o, f, 1, 1).wait_send()
+        sibling(2 * s - 1, o, core).wait_send()
+        sibling(2 * s, o, core).wait_send()
+
+    for f in range(2):
+        ring(0, half_z, 0, f, 1, 1).wait_send()
+        ring(1, half_z, 1, f, 1, 1).wait_send()
+    for o in range(2):
+        sibling(0, o, core).wait_send()
+        sibling(n_z - 1, o, core).wait_send()
+    for n in (0, 1, 2, 5, 6):
+        w_copy(n, own_w, own_w, dev_up).wait_send()
+    for n in (3, 4, 7, 8):
+        w_copy(n, w_half(x_hi, y, 0), w_half(x_hi, y, 0), dev_up).wait_send()
+    for n in range(9, 16):
+        w_sibling(n, x_hi, y, core).wait_send()
+
+    for i in range(1, n_heads):
+        t_arrival(lax.rem(head + i, n_heads)).wait_recv()
 
     counted = window_start(group + 1) - window_start(group)
     row_id = lax.broadcasted_iota(jnp.int32, (WINDOW, HEAD_DIM), 0)
@@ -420,11 +446,24 @@
         lanes = jnp.where(row_id < counted, lanes, 0.0)
         curve = curve + jnp.sum(lanes.reshape(WINDOW // 8, 8, HEAD_DIM), axis=0)
 
+    red_z[z, 0:8] = curve
+    red_z[z, 8:16] = residual_part
+
+    def red_copy(buf, here, n, base, device):
+        return remote(buf.at[here], buf.at[here], red_send.at[n], red_recv.at[base + here], device)
+
+    def red_arrival(buf, there, base):
+        return remote(buf.at[there], buf.at[there], red_send.at[0], red_recv.at[base + there], dev_pair)
+
+    for i in range(1, n_z):
+        other = lax.rem(z + i, n_z)
+        red_copy(red_z, z, i, 0, (group, at_ctx(other, x_lo, core))).start()
+
     def c_copy(h_):
         return remote(
             cout.at[:, head_cols(h_)], cin.at[x_lo, group],
             c_send.at[h_], c_recv.at[x_lo * n_group + group],
-            (lax.div(h_, 2), at_ctx(z, lax.rem(h_, 2), core)),
+            (h_ // 2, at_ctx(z, h_ % 2, core)),
         )
 
     def c_arrival(x_lo_, group_):
@@ -438,32 +477,22 @@
         at = slice(n * block, (n + 1) * block)
         cout[:, at] = dot_nt(plow[...], wbuf[at]).astype(BF16)
 
-        @pl.loop(n * (block // HEAD_DIM), (n + 1) * (block // HEAD_DIM))
-        def _(h_):
+        for h_ in range(n * (block // HEAD_DIM), (n + 1) * (block // HEAD_DIM)):
+
             @pl.when(h_ != head)
             def _():
                 c_copy(h_).start()
 
     cin[x_lo, group] = cout[:, head_cols(head)]
 
-    red_z[z, 0:8] = curve
-    red_z[z, 8:16] = residual_part
-
-    @pl.loop(1, n_z)
-    def _(i):
-        other = lax.rem(z + i, n_z)
-        remote(
-            red_z.at[z], red_z.at[z], red_send.at[i], red_recv.at[z],
-            (group, at_ctx(other, x_lo, core)),
-        ).start()
-
-    @pl.loop(0, 2 * n_group)
-    def _(i):
-        x_lo_, group_ = lax.div(i, n_group), lax.rem(i, n_group)
-
-        @pl.when(i != x_lo * n_group + group)
-        def _():
-            c_arrival(x_lo_, group_).wait_recv()
+    t_copy(group, 1 - x_lo, 0).wait_send()
+    for i in range(2, n_heads):
+        t_copy(0, 0, i).wait_send()
+
+    for i in range(1, n_group):
+        c_arrival(x_lo, lax.rem(group + i, n_group)).wait_recv()
+    for i in range(n_group):
+        c_arrival(1 - x_lo, i).wait_recv()
 
     starts = [((both // 16 - 3) * i + 3) // (n_group - 1) * 16 for i in range(n_group)]
     for i in range(n_group):
@@ -487,44 +516,15 @@
     def _(h):
         backward(h)
 
-    def red_arrival(buf, i, base):
-        return remote(buf.at[i], buf.at[i], red_send.at[0], red_recv.at[base + i], dev_pair)
-
-    @pl.loop(1, n_z)
-    def _(i):
+    for i in range(1, n_z):
         red_arrival(red_z, lax.rem(z + i, n_z), 0).wait_recv()
-
-    red_g[group] = jnp.sum(red_z[...], axis=0)
-
-    @pl.loop(1, n_group)
-    def _(i):
-        other = lax.rem(group + i, n_group)
-        remote(
-            red_g.at[group], red_g.at[group], red_send.at[n_z + i], red_recv.at[n_z + group],
-            (other, ctx),
-        ).start()
-
-    @pl.loop(6, 11)
-    def _(h):
-        backward(h)
-
-    @pl.loop(1, n_group)
-    def _(i):
-        red_arrival(red_g, lax.rem(group + i, n_group), n_z).wait_recv()
-
-    place = 2 * x_lo + core
-    red_c[place] = jnp.sum(red_g[...], axis=0)
-
-    @pl.loop(1, 4)
-    def _(i):
-        other = lax.rem(place + i, 4)
-        remote(
-            red_c.at[place], red_c.at[place],
-            red_send.at[n_z + n_group + i], red_recv.at[n_z + n_group + place],
-            (group, 4 * z + other),
-        ).start()
-
-    @pl.loop(11, n_units)
+    red_g[head] = jnp.sum(red_z[...], axis=0)
+    for i in range(1, n_heads):
+        other = lax.rem(head + i, n_heads)
+        device = (lax.div(other, 2), at_ctx(z, lax.rem(other, 2), core))
+        red_copy(red_g, head, n_z + i, n_z, device).start()
+
+    @pl.loop(6, n_units)
     def _(h):
         backward(h)
 
@@ -535,10 +535,23 @@
     )
     back_copy.start()
 
-    @pl.loop(1, 4)
-    def _(i):
-        red_arrival(red_c, lax.rem(place + i, 4), n_z + n_group).wait_recv()
-
+    for i in range(1, n_heads):
+        red_arrival(red_g, lax.rem(head + i, n_heads), n_z).wait_recv()
+    red_c[core] = jnp.sum(red_g[...], axis=0)
+    last = red_copy(red_c, core, n_z + n_heads, n_z + n_heads, dev_sib)
+    last.start()
+    for i in range(1, n_z):
+        red_copy(red_z, z, i, 0, dev_next).wait_send()
+    for i in range(1, n_heads):
+        red_copy(red_g, head, n_z + i, n_z, dev_pair).wait_send()
+    for h_ in range(n_heads):
+
+        @pl.when(h_ != head)
+        def _():
+            c_copy(h_).wait_send()
+
+    red_arrival(red_c, 1 - core, n_z + n_heads).wait_recv()
+    last.wait_send()
     sums = jnp.sum(red_c[...], axis=0)
     curvature = jnp.sum(jnp.sum(sums[0:8], axis=0, keepdims=True), axis=1, keepdims=True)
     residual_sq = jnp.sum(jnp.sum(sums[8:16], axis=0, keepdims=True), axis=1, keepdims=True)
@@ -546,56 +559,7 @@
     out_ref[:, own_cols] = dirb[:, own_cols].astype(F32) - step_size * qg[own_rows]
     back_copy.wait_recv()
     out_ref[:, other_cols] = dirb[:, other_cols].astype(F32) - step_size * qg_in[...]
-
     back_copy.wait_send()
-    for copy in swap:
-        copy.wait_send()
-
-    @pl.loop(0, 2 * (half_z - 1))
-    def _(i):
-        s, o = lax.div(i, 2) + 1, lax.rem(i, 2)
-        ring(0, s, o, 1, 1).wait_send()
-        ring(1, s, o, 1, 1).wait_send()
-        sibling(2 * s - 1, o, core).wait_send()
-        sibling(2 * s, o, core).wait_send()
-
-    ring(0, half_z, 0, 1, 1).wait_send()
-    ring(1, half_z, 1, 1, 1).wait_send()
-    for o in range(2):
-        sibling(0, o, core).wait_send()
-        sibling(n_z - 1, o, core).wait_send()
-    for n in (0, 1, 2, 5, 6):
-        w_copy(n, own_w, own_w, dev_up).wait_send()
-    for n in (3, 4, 7, 8):
-        w_copy(n, w_half(x_hi, y, 0), w_half(x_hi, y, 0), dev_up).wait_send()
-    for n in range(9, 16):
-        w_sibling(n, x_hi, y, core).wait_send()
-    t_copy(group, 1 - x_lo, 0).wait_send()
-
-    @pl.loop(2, n_heads)
-    def _(i):
-        t_copy(0, 0, i).wait_send()
-
-    @pl.loop(0, n_heads)
-    def _(h_):
-        @pl.when(h_ != head)
-        def _():
-            c_copy(h_).wait_send()
-
-    def red_sent(buf, n):
-        remote(buf.at[0], buf.at[0], red_send.at[n], red_recv.at[0], dev_pair).wait_send()
-
-    @pl.loop(1, n_z)
-    def _(i):
-        red_sent(red_z, i)
-
-    @pl.loop(1, n_group)
-    def _(i):
-        red_sent(red_g, n_z + i)
-
-    @pl.loop(1, 4)
-    def _(i):
-        red_sent(red_c, n_z + n_group + i)
 
 
 def body(n_group, n_z, queries, key_rows, value_rows, query_dir, out_weight):
@@ -605,7 +569,7 @@
     n_heads = 2 * n_group
     any_spec = pl.BlockSpec(memory_space=pl.ANY)
     dma = pltpu.SemaphoreType.DMA
-    n_red = n_z + n_group + 4
+    n_red = n_z + n_heads + 2
     return pl.pallas_call(
         functools.partial(kernel, n_group, n_z, rows),
         out_shape=jax.ShapeDtypeStruct((rows, 2 * HEAD_DIM), F32),
@@ -630,11 +594,11 @@
             pltpu.VMEM((both, HEAD_DIM), F32),
             pltpu.VMEM((rows, HEAD_DIM), F32),
             pltpu.VMEM((n_z, 16, HEAD_DIM), F32),
-            pltpu.VMEM((n_group, 16, HEAD_DIM), F32),
-            pltpu.VMEM((4, 16, HEAD_DIM), F32),
+            pltpu.VMEM((n_heads, 16, HEAD_DIM), F32),
+            pltpu.VMEM((2, 16, HEAD_DIM), F32),
             dma((6,)),
             dma((4,)), dma((4,)),
-            dma((2, n_z // 2, 2)), dma((2, n_z // 2, 2)),
+            dma((2, n_z // 2, 2, 2)), dma((2, n_z // 2, 2, 2)),
             dma((n_z, 2)), dma((n_z, 2)),
             dma((16,)), dma((16,)),
             dma((n_heads,)), dma((n_heads,)),

time: 91.7 us -> 82.8 us (0.903)
  Pallas kernels: 88.7 us -> 80.3 us
    pallas_call x1, Pallas kernels: 88.7 us -> 80.3 us  [body(): pl.pallas_call(functools.partial(kernel, n_group, n_z, rows), out_shape=j...]
where the time goes in v2:
time: 82.8 us; the launch traced here: 81.9 us
  Pallas kernels  80.3 us (97%)
  local copies, waits for them, and re-layouts  1.61 us (2%)
    pallas_call x1, Pallas kernels, body(): pl.pallas_call(functools.partial(kernel, n_group, n_z, rows), out_shape=j...  80.3 us

profile of v2, /device:TPU:1, one launch (start us, length us, event | category | flops | bytes accessed | tf_op | source)
XLA Modules:
  0.0 81.9 jit_solution(801446232547570727)
XLA Ops:
  0.0 80.3 %gauss_newton_layer.1 = f32[176,256]{1,0:T(8,128)} custom-call(bf16[176,256]{1,0:T(8,128)(2,1)} %q_ref.1, bf16[176,256]{1,0:T(8,128)(2,1)} %k_ref.1, bf16[176,256]{1,0:T(8,128)(2,1)} %v_ref.1, bf16[176,256]{1,0:T(8,128)(2,1)} %d_ref.1, bf16[256,3072]{1,0:T(8,128)(2,1)} %w_ref.1), custom_call_target="tpu_custom_call" | custom-call | tf_op jit(solution)/shard_map/gauss_newton_layer/pallas_call | solution.py:573
  80.3 1.6 %copy.7 = f32[176,256]{1,0:T(8,128)} copy(f32[176,256]{1,0:T(8,128)} %gauss_newton_layer.1) | data formatting | bytes 360448

commit v3 on v2

v3 whole, which is shorter than its diff:
```python
import functools
import math

import jax
import jax.numpy as jnp
from jax import lax
from jax.experimental import pallas as pl
from jax.experimental.pallas import tpu as pltpu
from jax.sharding import PartitionSpec as P

MESH = pl.DeviceIdType.MESH
HEAD_DIM = 128
SCALING = HEAD_DIM ** (-0.5)
EXP2_SCALE = SCALING * math.log2(math.e)
N_Y, N_XLO, N_CORE = 4, 2, 2
WINDOW = 48
F32, BF16 = jnp.float32, jnp.bfloat16


def dot_nt(a, b):
    return lax.dot_general(a, b, (((1,), (1,)), ((), ())), preferred_element_type=F32)


def dot_nn(a, b):
    return lax.dot_general(a, b, (((1,), (0,)), ((), ())), preferred_element_type=F32)


def kernel(
    n_group, n_z, rows,
    q_ref, k_ref, v_ref, d_ref, w_ref, out_ref,
    kb, vb, qd, pw, highs, high, acc, dirb, att, tbuf, tin, wbuf, plow, cout, cin, cbuf, qg, qg_in,
    red_z, red_g, red_c,
    local_sem, swap_send, swap_recv, ring_send, ring_recv, sib_send, sib_recv,
    w_send, w_recv, t_send, t_recv, c_send, c_recv, red_send, red_recv, back_send, back_recv,
):
    group, ctx = lax.axis_index("group"), lax.axis_index("ctx")
    x_hi, y = lax.div(group, N_Y), lax.rem(group, N_Y)
    z, x_lo, core = lax.div(ctx, 4), lax.rem(lax.div(ctx, 2), 2), lax.rem(ctx, 2)
    head = 2 * group + x_lo
    both = 2 * rows
    unit = 4 * rows
    half_z = n_z // 2
    n_heads = 2 * n_group
    wide = wbuf.shape[1]

    def at_ctx(z_, x_lo_, core_):
        return 4 * z_ + 2 * x_lo_ + core_

    z_next, z_prev = lax.rem(z + 1, n_z), lax.rem(z + n_z - 1, n_z)
    dev_next = (group, at_ctx(z_next, x_lo, core))
    dev_prev = (group, at_ctx(z_prev, x_lo, core))
    dev_sib = (group, at_ctx(z, x_lo, 1 - core))
    dev_pair = (group, at_ctx(z, 1 - x_lo, core))
    dev_across = ((1 - x_hi) * N_Y + y, at_ctx(z, 1 - x_lo, core))
    y_next, y_prev = lax.rem(y + 1, N_Y), lax.rem(y + N_Y - 1, N_Y)
    dev_up = (x_hi * N_Y + y_next, ctx)
    dev_down = (x_hi * N_Y + y_prev, ctx)

    def remote(src, dst, send, recv, device):
        return pltpu.make_async_remote_copy(
            src_ref=src, dst_ref=dst, send_sem=send, recv_sem=recv,
            device_id=device, device_id_type=MESH,
        )

    def own_plane_rows(j):
        return pl.ds(pl.multiple_of(core * both + j * rows, 16), rows)

    own_cols = pl.ds(pl.multiple_of(x_lo * HEAD_DIM, HEAD_DIM), HEAD_DIM)
    other_cols = pl.ds(pl.multiple_of((1 - x_lo) * HEAD_DIM, HEAD_DIM), HEAD_DIM)
    own_rows = pl.ds(pl.multiple_of(x_lo * rows, 16), rows)
    other_rows = pl.ds(pl.multiple_of((1 - x_lo) * rows, 16), rows)
    own_tan = pl.ds(pl.multiple_of(both + x_lo * rows, 16), rows)
    other_tan = pl.ds(pl.multiple_of(both + (1 - x_lo) * rows, 16), rows)
    first = own_plane_rows(x_lo)
    second = own_plane_rows(1 - x_lo)
    own_half = pl.ds(pl.multiple_of(x_lo * wide, 128), wide)
    other_half = pl.ds(pl.multiple_of((1 - x_lo) * wide, 128), wide)

    def w_rows(x_hi_, y_, piece):
        start = (x_hi_ * N_Y + y_) * 256 + piece * 128
        return pl.ds(pl.multiple_of(start, 128), 128)

    local = [
        pltpu.make_async_copy(k_ref.at[:, own_cols], kb.at[first], local_sem.at[0]),
        pltpu.make_async_copy(
            v_ref.at[:, own_cols], vb.at[first], local_sem.at[1]
        ),
        pltpu.make_async_copy(q_ref.at[:, own_cols], qd.at[own_rows], local_sem.at[2]),
        pltpu.make_async_copy(d_ref.at[:, own_cols], qd.at[own_tan], local_sem.at[3]),
        pltpu.make_async_copy(d_ref, dirb, local_sem.at[4]),
        pltpu.make_async_copy(
            w_ref.at[:, own_half],
            wbuf.at[pl.ds(pl.multiple_of(group * 256, 256), 256)],
            local_sem.at[5],
        ),
    ]
    for copy in local:
        copy.start()

    barrier = pltpu.get_barrier_semaphore()

    def greet(device):
        pl.semaphore_signal(barrier, inc=1, device_id=device, device_id_type=MESH)

    greet(dev_next)
    greet(dev_prev)
    greet(dev_sib)
    greet(dev_pair)
    for i in range(1, n_group):
        other = lax.rem(group + i, n_group)
        greet((other, at_ctx(z, x_lo, core)))
        greet((other, at_ctx(z, 1 - x_lo, core)))
    high[...] = jnp.full(high.shape, -1e30, F32)
    acc[...] = jnp.zeros(acc.shape, F32)
    qg[...] = jnp.zeros(qg.shape, F32)
    pl.semaphore_wait(barrier, 4 + 2 * (n_group - 1))

    swap = [
        remote(
            k_ref.at[:, other_cols], kb.at[first],
            swap_send.at[0], swap_recv.at[0], dev_pair,
        ),
        remote(
            v_ref.at[:, other_cols], vb.at[first],
            swap_send.at[1], swap_recv.at[1], dev_pair,
        ),
        remote(
            q_ref.at[:, other_cols], qd.at[own_rows], swap_send.at[2], swap_recv.at[2], dev_pair
        ),
        remote(
            d_ref.at[:, other_cols], qd.at[own_tan], swap_send.at[3], swap_recv.at[3], dev_pair
        ),
    ]
    swap_in = [
        remote(
            k_ref.at[:, other_cols], kb.at[second],
            swap_send.at[0], swap_recv.at[0], dev_pair,
        ),
        remote(
            v_ref.at[:, other_cols], vb.at[second],
            swap_send.at[1], swap_recv.at[1], dev_pair,
        ),
        remote(
            q_ref.at[:, other_cols], qd.at[other_rows], swap_send.at[2], swap_recv.at[2], dev_pair
        ),
        remote(
            d_ref.at[:, other_cols], qd.at[other_tan], swap_send.at[3], swap_recv.at[3], dev_pair
        ),
    ]
    swap[0].start()
    swap[1].start()

    part_start, part_step = x_lo * rows, (1 - 2 * x_lo) * rows
    mine = core * both
    theirs = (1 - core) * both

    def rows_at(way, s, o, offset):
        base = s * (2 * unit) + part_start + o * part_step + offset
        if way == 0:
            base = base - unit
        return pl.ds(pl.multiple_of(base, 16), rows)

    def ring(way, s, o, f, src, dst):
        buf = (kb, vb)[f]
        n = s * 8 + (way * 4 + o * 2 + f)
        return remote(
            buf.at[src], buf.at[dst], ring_send.at[n], ring_recv.at[n],
            dev_next if way == 0 else dev_prev,
        )

    def ring_start(way, s, o, f):
        src = rows_at(1, s - 1, o, mine) if way else rows_at(0, s - 1, o, mine)
        ring(way, s, o, f, src, rows_at(way, s, o, mine)).start()

    def ring_first(way, o, f):
        if o == 0:
            n = 8 + way * 4 + f
            remote(
                (k_ref, v_ref)[f].at[:, own_cols], (kb, vb)[f].at[rows_at(way, 1, 0, mine)],
                ring_send.at[n], ring_recv.at[n], dev_next if way == 0 else dev_prev,
            ).start()
        else:
            ring(way, 1, o, f, rows_at(1, 0, o, mine), rows_at(way, 1, o, mine)).start()

    def ring_wait(way, s, o, f):
        place = rows_at(way, s, o, mine)
        ring(way, s, o, f, place, place).wait_recv()

    def last_start(way, f):
        src = rows_at(way, half_z - 1, way, mine)
        ring(way, half_z, way, f, src, rows_at(0, half_z, way, mine)).start()

    def last_wait(way, f):
        place = rows_at(0, half_z, way, mine)
        ring(way, half_z, way, f, place, place).wait_recv()

    def sibling(p, f, offset):
        place = (kb, vb)[f].at[pl.ds(pl.multiple_of(p * unit + offset, 16), both)]
        return remote(place, place, sib_send.at[p * 2 + f], sib_recv.at[p * 2 + f], dev_sib)

    def sibling_part(p, o, f, offset):
        start = p * unit + part_start + o * part_step + offset
        place = (kb, vb)[f].at[pl.ds(pl.multiple_of(start, 16), rows)]
        n = 2 * n_z + (o * 2 + f if p else 4 + o * 2 + f)
        return remote(place, place, sib_send.at[n], sib_recv.at[n], dev_sib)

    for f in range(2):
        ring_first(0, 0, f)
        ring_first(1, 0, f)
    swap[2].start()
    swap[3].start()
    for f in range(2):
        local[f].wait()
        sibling_part(0, 0, f, mine).start()

    def w_copy(n, src, dst, device):
        return remote(src, dst, w_send.at[n], w_recv.at[n], device)

    def w_piece(x_hi_, y_, piece):
        return wbuf.at[w_rows(x_hi_, y_, piece)]

    def w_half(x_hi_, y_, part):
        start = (x_hi_ * N_Y + y_) * 256 + core * 128 + part * 64
        return wbuf.at[pl.ds(pl.multiple_of(start, 64), 64)]

    y_far = lax.rem(y + 2, N_Y)
    def w_src(q):
        return w_ref.at[pl.ds(pl.multiple_of(core * 128 + q * 64, 64), 64), other_half]

    def w_own(q):
        return w_ref.at[pl.ds(pl.multiple_of(core * 128 + q * 64, 64), 64), own_half]

    for q in range(2):
        w_copy(q, w_src(q), w_half(x_hi, y, q), dev_across).start()
        w_copy(2 + q, w_own(q), w_half(x_hi, y, q), dev_up).start()
        w_copy(4 + q, w_own(1 - q), w_half(x_hi, y, 1 - q), dev_down).start()

    for f in range(2):
        swap_in[f].wait_recv()
        ring_first(0, 1, f)
        ring_first(1, 1, f)
    for f in range(2):
        sibling_part(0, 1, f, mine).start()

    def w_sibling(n, x_hi_, y_, core_):
        place = w_piece(x_hi_, y_, core_)
        return w_copy(n, place, place, dev_sib)

    def w_take(n, x_hi_, y_, part):
        place = w_half(x_hi_, y_, part)
        w_copy(n, place, place, dev_up).wait_recv()

    def w_give(n, x_hi_, y_, part, device):
        place = w_half(x_hi_, y_, part)
        w_copy(n, place, place, device).start()

    x_not = 1 - x_hi

    def w_first():
        w_take(0, x_not, y, 0)
        w_give(8, x_not, y, 0, dev_up)
        w_take(2, x_hi, y_prev, 0)
        w_give(6, x_hi, y_prev, 0, dev_up)
        w_take(4, x_hi, y_next, 1)
        w_give(7, x_hi, y_next, 1, dev_down)

    def w_second():
        w_take(1, x_not, y, 1)
        w_give(10, x_not, y, 1, dev_down)
        w_give(9, x_not, y, 1, dev_up)
        w_give(11, x_not, y, 0, dev_down)
        w_sibling(14, x_not, y, core).start()
        w_take(3, x_hi, y_prev, 1)
        w_sibling(15, x_hi, y_prev, core).start()
        w_take(5, x_hi, y_next, 0)
        w_sibling(16, x_hi, y_next, core).start()

    def w_third():
        w_take(8, x_not, y_prev, 0)
        w_give(12, x_not, y_prev, 0, dev_up)
        w_take(10, x_not, y_next, 1)
        w_give(13, x_not, y_next, 1, dev_down)
        w_take(6, x_hi, y_far, 0)
        w_take(7, x_hi, y_far, 1)
        w_sibling(17, x_hi, y_far, core).start()

    def w_fourth():
        w_take(9, x_not, y_prev, 1)
        w_sibling(18, x_not, y_prev, core).start()
        w_take(11, x_not, y_next, 0)
        w_sibling(19, x_not, y_next, core).start()
        w_take(12, x_not, y_far, 0)
        w_take(13, x_not, y_far, 1)
        w_sibling(20, x_not, y_far, core).start()

    def w_finish():
        local[5].wait()
        w_sibling(14, x_not, y, 1 - core).wait_recv()
        w_sibling(15, x_hi, y_prev, 1 - core).wait_recv()
        w_sibling(16, x_hi, y_next, 1 - core).wait_recv()
        w_sibling(17, x_hi, y_far, 1 - core).wait_recv()
        w_sibling(18, x_not, y_prev, 1 - core).wait_recv()
        w_sibling(19, x_not, y_next, 1 - core).wait_recv()
        w_sibling(20, x_not, y_far, 1 - core).wait_recv()

    def when(condition):
        if isinstance(condition, bool):
            return lambda run: run() if condition else None
        return pl.when(condition)

    def service(s, o):
        def ways(final):
            for f in range(2):
                for way in range(2):
                    ring_wait(way, s, o, f)
                    if final:

                        @when(o == way)
                        def _():
                            last_start(way, f)

                    else:
                        ring_start(way, s + 1, o, f)

            @when(o == 1)
            def _():
                for way in range(2):
                    for f in range(2):
                        sibling(2 * s - 1 + way, f, mine).start()

        @when(s < half_z - 1)
        def _():
            ways(False)

        @when(s == half_z - 1)
        def _():
            ways(True)

        @when(s == half_z)
        def _():
            for f in range(2):
                for way in range(2):

                    @when(o == way)
                    def _():
                        last_wait(way, f)
                        sibling_part(n_z - 1, way, f, mine).start()

    def unit_rows(h):
        return pl.ds(pl.multiple_of(h * unit, 16), unit)

    ones = jnp.ones((unit, HEAD_DIM), BF16)

    def forward(units):
        blocks = []
        for h in units:
            keys = kb[unit_rows(h)]
            blocks.append((dot_nt(qd[0:both], keys), dot_nt(qd[both : 2 * both], keys)))
        old = high[...]
        new = old
        for scores, _ in blocks:
            new = jnp.maximum(new, jnp.max(scores, axis=1, keepdims=True))
        high[...] = new
        factor = jnp.exp2((old - new) * EXP2_SCALE)
        mixed = tangent_mixed = None
        for h, (scores, tangents) in zip(units, blocks):
            weights = jnp.exp2((scores - new) * EXP2_SCALE)
            weighted = (weights * tangents).astype(BF16)
            weights = weights.astype(BF16)
            highs[h] = new
            pw[h] = weights
            values = jnp.concatenate([vb[unit_rows(h)], ones], axis=1)
            a, b = dot_nn(weights, values), dot_nn(weighted, values)
            mixed = a if mixed is None else mixed + a
            tangent_mixed = b if tangent_mixed is None else tangent_mixed + b
        acc[0:both] = acc[0:both] * factor + mixed
        acc[both : 2 * both] = acc[both : 2 * both] * factor + tangent_mixed

    n_units = n_z
    service(1, 0)
    for copy in local[2:5]:
        copy.wait()
    swap_in[2].wait_recv()
    swap_in[3].wait_recv()
    direction = dirb[...].astype(F32)
    squares = jnp.sum((direction * direction).reshape(rows // 8, 8, 2 * HEAD_DIM), axis=0)
    residual_part = squares[:, :HEAD_DIM] + squares[:, HEAD_DIM:]
    for o in range(2):
        for f in range(2):
            sibling_part(0, o, f, theirs).wait_recv()

    service(1, 1)

    @pl.loop(2, half_z + 2)
    def _(s):
        @pl.when(s <= half_z)
        def _():
            service(s, 0)

        @pl.when(s > 2)
        def _():
            for f in range(2):
                sibling(2 * s - 4, f, theirs).wait_recv()

        @pl.when(s <= half_z)
        def _():
            for f in range(2):
                sibling(2 * s - 3, f, theirs).wait_recv()

        @pl.when(s > half_z)
        def _():
            for o in range(2):
                for f in range(2):
                    sibling_part(n_z - 1, o, f, theirs).wait_recv()

        forward([2 * s - 4, 2 * s - 3])

        @pl.when(s == 3)
        def _():
            w_first()

        @pl.when(s == 4)
        def _():
            w_second()

        @pl.when(s == 6)
        def _():
            w_third()

        @pl.when(s == half_z)
        def _():
            w_fourth()

        @pl.when(s <= half_z)
        def _():
            service(s, 1)

    totals = acc[0:both, HEAD_DIM : 2 * HEAD_DIM]
    attended = acc[0:both, 0:HEAD_DIM] / totals
    tbuf[...] = (
        (acc[both : 2 * both, 0:HEAD_DIM] - acc[both : 2 * both, HEAD_DIM : 2 * HEAD_DIM] * attended)
        * (SCALING / totals)
    ).astype(BF16)

    def window_start(i):
        return lax.div(((both // 16 - 3) * i + 3), n_group - 1) * 16

    def window(i):
        return pl.ds(pl.multiple_of(window_start(i), 16), WINDOW)

    def head_cols(h_):
        return pl.ds(pl.multiple_of(h_ * HEAD_DIM, HEAD_DIM), HEAD_DIM)

    def t_copy(group_, x_lo_, slot):
        return remote(
            tbuf.at[window(group_)], tin.at[:, head_cols(head)],
            t_send.at[slot], t_recv.at[head], (group_, at_ctx(z, x_lo_, core)),
        )

    def t_arrival(h_):
        return remote(
            tbuf.at[window(0)], tin.at[:, head_cols(h_)], t_send.at[0], t_recv.at[h_], dev_pair
        )

    t_copy(group, 1 - x_lo, 0).start()
    for i in range(1, n_group):
        other = lax.rem(group + i, n_group)
        t_copy(other, x_lo, 2 * i).start()
        t_copy(other, 1 - x_lo, 2 * i + 1).start()

    tin[:, head_cols(head)] = tbuf[window(group)]
    att[...] = attended
    w_finish()

    for copy in swap:
        copy.wait_send()

    def left(size, sem):
        remote(kb.at[0:size], kb.at[0:size], sem, ring_recv.at[0], dev_next).wait_send()

    for s in range(1, half_z):
        for n in range(8):
            left(rows, ring_send.at[s * 8 + n])
    for way in range(2):
        for f in range(2):
            left(rows, ring_send.at[half_z * 8 + way * 6 + f])
            left(rows, sib_send.at[2 * n_z + way * 2 + f])
            left(rows, sib_send.at[2 * n_z + 4 + way * 2 + f])
    for n in range(2, 2 * n_z - 2):
        left(both, sib_send.at[n])
    for n in range(14):
        w_copy(n, w_half(x_hi, y, 0), w_half(x_hi, y, 0), dev_up).wait_send()
    for n in range(14, 21):
        w_sibling(n, x_hi, y, core).wait_send()

    for i in range(1, n_heads):
        t_arrival(lax.rem(head + i, n_heads)).wait_recv()

    counted = window_start(group + 1) - window_start(group)
    row_id = lax.broadcasted_iota(jnp.int32, (WINDOW, HEAD_DIM), 0)
    curve = jnp.zeros((8, HEAD_DIM), F32)
    step = wide // 3
    for n in range(3):
        cols = slice(n * step, (n + 1) * step)
        proj = dot_nn(tin[...], wbuf[:, cols])
        plow[:, cols] = proj.astype(BF16)
        squared = proj * proj
        lanes = squared[:, 0:HEAD_DIM]
        for m in range(1, step // HEAD_DIM):
            lanes = lanes + squared[:, m * HEAD_DIM : (m + 1) * HEAD_DIM]
        lanes = jnp.where(row_id < counted, lanes, 0.0)
        curve = curve + jnp.sum(lanes.reshape(WINDOW // 8, 8, HEAD_DIM), axis=0)

    red_z[z, 0:8] = curve
    red_z[z, 8:16] = residual_part

    def red_copy(buf, here, n, base, device):
        return remote(buf.at[here], buf.at[here], red_send.at[n], red_recv.at[base + here], device)

    def red_arrival(buf, there, base):
        return remote(buf.at[there], buf.at[there], red_send.at[0], red_recv.at[base + there], dev_pair)

    for i in range(1, n_z):
        other = lax.rem(z + i, n_z)
        red_copy(red_z, z, i, 0, (group, at_ctx(other, x_lo, core))).start()

    def c_copy(h_):
        return remote(
            cout.at[:, head_cols(h_)], cin.at[x_lo, group],
            c_send.at[h_], c_recv.at[x_lo * n_group + group],
            (h_ // 2, at_ctx(z, h_ % 2, core)),
        )

    def c_arrival(x_lo_, group_):
        return remote(
            cout.at[:, head_cols(0)], cin.at[x_lo_, group_],
            c_send.at[0], c_recv.at[x_lo_ * n_group + group_], dev_pair,
        )

    block = 512
    for n in range(n_heads * HEAD_DIM // block):
        at = slice(n * block, (n + 1) * block)
        cout[:, at] = dot_nt(plow[...], wbuf[at]).astype(BF16)

        for h_ in range(n * (block // HEAD_DIM), (n + 1) * (block // HEAD_DIM)):

            @pl.when(h_ != head)
            def _():
                c_copy(h_).start()

    cin[x_lo, group] = cout[:, head_cols(head)]

    t_copy(group, 1 - x_lo, 0).wait_send()
    for i in range(2, n_heads):
        t_copy(0, 0, i).wait_send()

    for i in range(1, n_group):
        c_arrival(x_lo, lax.rem(group + i, n_group)).wait_recv()
    for i in range(n_group):
        c_arrival(1 - x_lo, i).wait_recv()

    starts = [((both // 16 - 3) * i + 3) // (n_group - 1) * 16 for i in range(n_group)]
    for i in range(n_group):
        cbuf[starts[i] : starts[i] + WINDOW] = (
            cin[0, i].astype(F32) + cin[1, i].astype(F32)
        ).astype(BF16)

    def backward(first_unit, block_rows):
        cot = cbuf[block_rows]
        centering = jnp.sum(cot.astype(F32) * att[block_rows], axis=1, keepdims=True)
        final = high[block_rows]
        units = [first_unit + i for i in range(4)]
        backs = [dot_nt(cot, vb[unit_rows(h)]) for h in units]
        total = None
        for h, back in zip(units, backs):
            grad = (pw[h, block_rows].astype(F32) * (back - centering)).astype(BF16)
            factor = jnp.exp2((highs[h, block_rows] - final) * EXP2_SCALE)
            product = dot_nn(grad, kb[unit_rows(h)]) * factor
            total = product if total is None else total + product
        qg[block_rows] += total

    def scaled(block_rows):
        return qg[block_rows] * (SCALING / acc[block_rows, HEAD_DIM : 2 * HEAD_DIM])

    @pl.loop(0, n_units // 8)
    def _(i):
        backward(4 * i, other_rows)

    for i in range(1, n_z):
        red_arrival(red_z, lax.rem(z + i, n_z), 0).wait_recv()
    red_g[head] = jnp.sum(red_z[...], axis=0)
    for i in range(1, n_heads):
        other = lax.rem(head + i, n_heads)
        device = (lax.div(other, 2), at_ctx(z, lax.rem(other, 2), core))
        red_copy(red_g, head, n_z + i, n_z, device).start()

    @pl.loop(n_units // 8, n_units // 4)
    def _(i):
        backward(4 * i, other_rows)

    qg[other_rows] = scaled(other_rows)
    back_copy = remote(
        qg.at[other_rows], qg_in, back_send.at[0], back_recv.at[0], dev_pair
    )
    back_copy.start()

    @pl.loop(0, n_units // 4)
    def _(i):
        backward(4 * i, own_rows)


    for i in range(1, n_heads):
        red_arrival(red_g, lax.rem(head + i, n_heads), n_z).wait_recv()
    red_c[core] = jnp.sum(red_g[...], axis=0)
    last = red_copy(red_c, core, n_z + n_heads, n_z + n_heads, dev_sib)
    last.start()
    for i in range(1, n_z):
        red_copy(red_z, z, i, 0, dev_next).wait_send()
    for i in range(1, n_heads):
        red_copy(red_g, head, n_z + i, n_z, dev_pair).wait_send()
    for h_ in range(n_heads):

        @pl.when(h_ != head)
        def _():
            c_copy(h_).wait_send()

    red_arrival(red_c, 1 - core, n_z + n_heads).wait_recv()
    last.wait_send()
    sums = jnp.sum(red_c[...], axis=0)
    curvature = jnp.sum(jnp.sum(sums[0:8], axis=0, keepdims=True), axis=1, keepdims=True)
    residual_sq = jnp.sum(jnp.sum(sums[8:16], axis=0, keepdims=True), axis=1, keepdims=True)
    step_size = residual_sq / curvature
    out_ref[:, own_cols] = dirb[:, own_cols].astype(F32) - step_size * scaled(own_rows)
    back_copy.wait_recv()
    out_ref[:, other_cols] = dirb[:, other_cols].astype(F32) - step_size * qg_in[...]
    back_copy.wait_send()


def body(n_group, n_z, queries, key_rows, value_rows, query_dir, out_weight):
    rows = queries.shape[0]
    both, unit = 2 * rows, 4 * rows
    width = out_weight.shape[1]
    n_heads = 2 * n_group
    any_spec = pl.BlockSpec(memory_space=pl.ANY)
    dma = pltpu.SemaphoreType.DMA
    n_red = n_z + n_heads + 2
    return pl.pallas_call(
        functools.partial(kernel, n_group, n_z, rows),
        out_shape=jax.ShapeDtypeStruct((rows, 2 * HEAD_DIM), F32),
        in_specs=[any_spec] * 5,
        out_specs=pl.BlockSpec(memory_space=pltpu.VMEM),
        scratch_shapes=[
            pltpu.VMEM((n_z * unit, HEAD_DIM), BF16),
            pltpu.VMEM((n_z * unit, HEAD_DIM), BF16),
            pltpu.VMEM((2 * both, HEAD_DIM), BF16),
            pltpu.VMEM((n_z, both, unit), BF16),
            pltpu.VMEM((n_z, both, 1), F32),
            pltpu.VMEM((both, 1), F32),
            pltpu.VMEM((2 * both, 2 * HEAD_DIM), F32),
            pltpu.VMEM((rows, 2 * HEAD_DIM), BF16),
            pltpu.VMEM((both, HEAD_DIM), F32),
            pltpu.VMEM((both, HEAD_DIM), BF16),
            pltpu.VMEM((WINDOW, n_heads * HEAD_DIM), BF16),
            pltpu.VMEM((n_heads * HEAD_DIM, width // 2), BF16),
            pltpu.VMEM((WINDOW, width // 2), BF16),
            pltpu.VMEM((WINDOW, n_heads * HEAD_DIM), BF16),
            pltpu.VMEM((2, n_group, WINDOW, HEAD_DIM), BF16),
            pltpu.VMEM((both, HEAD_DIM), BF16),
            pltpu.VMEM((both, HEAD_DIM), F32),
            pltpu.VMEM((rows, HEAD_DIM), F32),
            pltpu.VMEM((n_z, 16, HEAD_DIM), F32),
            pltpu.VMEM((n_heads, 16, HEAD_DIM), F32),
            pltpu.VMEM((2, 16, HEAD_DIM), F32),
            dma((6,)),
            dma((4,)), dma((4,)),
            dma((4 * n_z + 8,)), dma((4 * n_z + 8,)),
            dma((2 * n_z + 8,)), dma((2 * n_z + 8,)),
            dma((21,)), dma((21,)),
            dma((n_heads,)), dma((n_heads,)),
            dma((n_heads,)), dma((n_heads,)),
            dma((n_red,)), dma((n_red,)),
            dma((1,)), dma((1,)),
        ],
        compiler_params=pltpu.CompilerParams(
            collective_id=0, has_side_effects=True, vmem_limit_bytes=60 * 1024 * 1024
        ),
        name="gauss_newton_layer",
    )(queries, key_rows, value_rows, query_dir, out_weight)


def solution(mesh):
    n_group, n_ctx = mesh.shape["group"], mesh.shape["ctx"]
    in_specs = (
        P("ctx", "group"),
        P("ctx", "group"),
        P("ctx", "group"),
        P("ctx", "group"),
        P("group", None),
    )
    return jax.shard_map(
        functools.partial(body, n_group, n_ctx // (N_XLO * N_CORE)),
        mesh=mesh, in_specs=in_specs, out_specs=P("ctx", "group"), check_vma=False,
    )
```

time: 82.8 us -> 87.2 us (1.053)
  Pallas kernels: 80.3 us -> 85.5 us
    pallas_call x1, Pallas kernels: 80.3 us -> 85.5 us  [body(): pl.pallas_call(functools.partial(kernel, n_group, n_z, rows), out_shape=j...]
where the time goes in v3:
time: 87.2 us; the launch traced here: 87.1 us
  Pallas kernels  85.5 us (98%)
  local copies, waits for them, and re-layouts  1.61 us (2%)
    pallas_call x1, Pallas kernels, body(): pl.pallas_call(functools.partial(kernel, n_group, n_z, rows), out_shape=j...  85.5 us

profile of v3, /device:TPU:1, one launch (start us, length us, event | category | flops | bytes accessed | tf_op | source)
XLA Modules:
  0.0 87.1 jit_solution(7534143029208703375)
XLA Ops:
  0.0 85.5 %gauss_newton_layer.1 = f32[176,256]{1,0:T(8,128)} custom-call(bf16[176,256]{1,0:T(8,128)(2,1)} %q_ref.1, bf16[176,256]{1,0:T(8,128)(2,1)} %k_ref.1, bf16[176,256]{1,0:T(8,128)(2,1)} %v_ref.1, bf16[176,256]{1,0:T(8,128)(2,1)} %d_ref.1, bf16[256,3072]{1,0:T(8,128)(2,1)} %w_ref.1), custom_call_target="tpu_custom_call" | custom-call | tf_op jit(solution)/shard_map/gauss_newton_layer/pallas_call | solution.py:647
  85.5 1.6 %copy.7 = f32[176,256]{1,0:T(8,128)} copy(f32[176,256]{1,0:T(8,128)} %gauss_newton_layer.1) | data formatting | bytes 360448

commit v4 on v2

--- a/solution.py
+++ b/solution.py
@@ -28,8 +28,8 @@
 def kernel(
     n_group, n_z, rows,
     q_ref, k_ref, v_ref, d_ref, w_ref, out_ref,
-    kv, qd, pw, highs, high, acc, dirb, att, tbuf, tin, wbuf, plow, cout, cin, cbuf, qg, qg_in,
-    red_z, red_g, red_c,
+    kv, qd, pw, highs, high, acc, dirb, att, tbuf, tin, wbuf, plow, cout, cin, cbuf, qg, qg_out, qg_in,
+    red_z, red_g, red_c, curve_sum,
     local_sem, swap_send, swap_recv, ring_send, ring_recv, sib_send, sib_recv,
     w_send, w_recv, t_send, t_recv, c_send, c_recv, red_send, red_recv, back_send, back_recv,
 ):
@@ -236,6 +236,16 @@
         w_copy(4, place, place, dev_down).wait_recv()
         w_sibling(12, x_hi, y_far, core).start()
 
+    def w_sent():
+        for copy in swap:
+            copy.wait_send()
+        for n in (0, 1, 2, 5, 6):
+            w_copy(n, own_w, own_w, dev_up).wait_send()
+        for n in (3, 4):
+            w_copy(n, w_half(x_hi, y, 0), w_half(x_hi, y, 0), dev_up).wait_send()
+        for n in range(9, 15):
+            w_sibling(n, x_hi, y, core).wait_send()
+
     def w_last():
         place = w_half(1 - x_hi, y_far, 0)
         w_copy(7, place, place, dev_up).wait_recv()
@@ -254,14 +264,7 @@
 
     high[...] = jnp.full(high.shape, -1e30, F32)
     acc[...] = jnp.zeros(acc.shape, F32)
-    for copy in local[2:5]:
-        copy.wait()
-    swap_in[2].wait_recv()
-    swap_in[3].wait_recv()
-    direction = dirb[...].astype(F32)
-    squares = jnp.sum((direction * direction).reshape(rows // 8, 8, 2 * HEAD_DIM), axis=0)
-    residual_part = squares[:, :HEAD_DIM] + squares[:, HEAD_DIM:]
-
+    qg[...] = jnp.zeros(qg.shape, F32)
     def service(h):
         b, o = lax.div(h, 2), lax.rem(h, 2)
         s = b + 1
@@ -308,6 +311,14 @@
                     ring(1, s, o, f, back_p, back_p).wait_recv()
 
             sibling(back_p, o, core).start()
+
+        @pl.when(s >= 2)
+        def _():
+            for f in range(2):
+                ring(0, s - 1, o, f, 1, 1).wait_send()
+                ring(1, s - 1, o, f, 1, 1).wait_send()
+            sibling(2 * s - 3, o, core).wait_send()
+            sibling(2 * s - 2, o, core).wait_send()
 
     def unit_rows(h):
         start = lax.div(h, 2) * (2 * unit) + part_of(lax.rem(h, 2)) * unit
@@ -348,10 +359,19 @@
 
     n_units = n_z
     service(0)
-
-    @pl.loop(1, n_units)
+    for copy in local[2:5]:
+        copy.wait()
+    swap_in[2].wait_recv()
+    swap_in[3].wait_recv()
+    direction = dirb[...].astype(F32)
+    squares = jnp.sum((direction * direction).reshape(rows // 8, 8, 2 * HEAD_DIM), axis=0)
+    residual_part = squares[:, :HEAD_DIM] + squares[:, HEAD_DIM:]
+
+    @pl.loop(1, n_units + 1)
     def _(h):
-        service(h)
+        @pl.when(h < n_units)
+        def _():
+            service(h)
 
         @pl.when(h == 5)
         def _():
@@ -361,14 +381,18 @@
         def _():
             w_late()
 
+        @pl.when(h == 14)
+        def _():
+            w_sent()
+
+        @pl.when(h == n_units)
+        def _():
+            w_last()
+
         forward(h - 1)
-
-    w_last()
-    forward(n_units - 1)
 
     totals = acc[0:both, HEAD_DIM : 2 * HEAD_DIM]
     attended = acc[0:both, 0:HEAD_DIM] / totals
-    att[...] = attended
     tbuf[...] = (
         (acc[both : 2 * both, 0:HEAD_DIM] - acc[both : 2 * both, HEAD_DIM : 2 * HEAD_DIM] * attended)
         * (SCALING / totals)
@@ -401,19 +425,8 @@
         t_copy(other, 1 - x_lo, 2 * i + 1).start()
 
     tin[:, head_cols(head)] = tbuf[window(group)]
+    att[...] = attended
     w_finish()
-
-    for copy in swap:
-        copy.wait_send()
-
-    @pl.loop(0, 2 * (half_z - 1))
-    def _(i):
-        s, o = lax.div(i, 2) + 1, lax.rem(i, 2)
-        for f in range(2):
-            ring(0, s, o, f, 1, 1).wait_send()
-            ring(1, s, o, f, 1, 1).wait_send()
-        sibling(2 * s - 1, o, core).wait_send()
-        sibling(2 * s, o, core).wait_send()
 
     for f in range(2):
         ring(0, half_z, 0, f, 1, 1).wait_send()
@@ -421,22 +434,21 @@
     for o in range(2):
         sibling(0, o, core).wait_send()
         sibling(n_z - 1, o, core).wait_send()
-    for n in (0, 1, 2, 5, 6):
-        w_copy(n, own_w, own_w, dev_up).wait_send()
-    for n in (3, 4, 7, 8):
+    for n in (7, 8):
         w_copy(n, w_half(x_hi, y, 0), w_half(x_hi, y, 0), dev_up).wait_send()
-    for n in range(9, 16):
-        w_sibling(n, x_hi, y, core).wait_send()
+    w_sibling(15, x_hi, y, core).wait_send()
 
     for i in range(1, n_heads):
         t_arrival(lax.rem(head + i, n_heads)).wait_recv()
 
     counted = window_start(group + 1) - window_start(group)
     row_id = lax.broadcasted_iota(jnp.int32, (WINDOW, HEAD_DIM), 0)
-    curve = jnp.zeros((8, HEAD_DIM), F32)
     step = wide // 3
-    for n in range(3):
-        cols = slice(n * step, (n + 1) * step)
+    curve_sum[...] = jnp.zeros(curve_sum.shape, F32)
+
+    @pl.loop(0, 3)
+    def _(n):
+        cols = pl.ds(pl.multiple_of(n * step, 128), step)
         proj = dot_nn(tin[...], wbuf[:, cols])
         plow[:, cols] = proj.astype(BF16)
         squared = proj * proj
@@ -444,9 +456,9 @@
         for m in range(1, step // HEAD_DIM):
             lanes = lanes + squared[:, m * HEAD_DIM : (m + 1) * HEAD_DIM]
         lanes = jnp.where(row_id < counted, lanes, 0.0)
-        curve = curve + jnp.sum(lanes.reshape(WINDOW // 8, 8, HEAD_DIM), axis=0)
-
-    red_z[z, 0:8] = curve
+        curve_sum[...] += jnp.sum(lanes.reshape(WINDOW // 8, 8, HEAD_DIM), axis=0)
+
+    red_z[z, 0:8] = curve_sum[...]
     red_z[z, 8:16] = residual_part
 
     def red_copy(buf, here, n, base, device):
@@ -463,7 +475,7 @@
         return remote(
             cout.at[:, head_cols(h_)], cin.at[x_lo, group],
             c_send.at[h_], c_recv.at[x_lo * n_group + group],
-            (h_ // 2, at_ctx(z, h_ % 2, core)),
+            (lax.div(h_, 2), at_ctx(z, lax.rem(h_, 2), core)),
         )
 
     def c_arrival(x_lo_, group_):
@@ -473,11 +485,14 @@
         )
 
     block = 512
-    for n in range(n_heads * HEAD_DIM // block):
-        at = slice(n * block, (n + 1) * block)
+
+    @pl.loop(0, n_heads * HEAD_DIM // block)
+    def _(n):
+        at = pl.ds(pl.multiple_of(n * block, block), block)
         cout[:, at] = dot_nt(plow[...], wbuf[at]).astype(BF16)
 
-        for h_ in range(n * (block // HEAD_DIM), (n + 1) * (block // HEAD_DIM)):
+        for i in range(block // HEAD_DIM):
+            h_ = n * (block // HEAD_DIM) + i
 
             @pl.when(h_ != head)
             def _():
@@ -499,22 +514,27 @@
         cbuf[starts[i] : starts[i] + WINDOW] = (
             cin[0, i].astype(F32) + cin[1, i].astype(F32)
         ).astype(BF16)
-    centering = jnp.sum(cbuf[...].astype(F32) * att[...], axis=1, keepdims=True)
-
-    qg[...] = jnp.zeros(qg.shape, F32)
-
-    def backward(h):
-        here = unit_rows(h)
-        keys = kv[here, 0:HEAD_DIM]
-        values = kv[here, HEAD_DIM : 2 * HEAD_DIM]
-        back = dot_nt(cbuf[...], values)
-        grad = (pw[h, 0:both].astype(F32) * (back - centering)).astype(BF16)
-        factor = jnp.exp2((highs[h] - high[...]) * EXP2_SCALE)
-        qg[...] += dot_nn(grad, keys) * factor
-
-    @pl.loop(0, 6)
-    def _(h):
-        backward(h)
+
+    def backward(first_unit, block_rows):
+        cot = cbuf[block_rows]
+        centering = jnp.sum(cot.astype(F32) * att[block_rows], axis=1, keepdims=True)
+        final = high[block_rows]
+        units = [first_unit + i for i in range(4)]
+        backs = [dot_nt(cot, kv[unit_rows(h), HEAD_DIM : 2 * HEAD_DIM]) for h in units]
+        total = None
+        for h, back in zip(units, backs):
+            grad = (pw[h, block_rows].astype(F32) * (back - centering)).astype(BF16)
+            factor = jnp.exp2((highs[h, block_rows] - final) * EXP2_SCALE)
+            product = dot_nn(grad, kv[unit_rows(h), 0:HEAD_DIM]) * factor
+            total = product if total is None else total + product
+        qg[block_rows] += total
+
+    def scaled(block_rows):
+        return qg[block_rows] * (SCALING / acc[block_rows, HEAD_DIM : 2 * HEAD_DIM])
+
+    back_copy = remote(qg_out, qg_in, back_send.at[0], back_recv.at[0], dev_pair)
+    last = red_copy(red_c, core, n_z + n_heads, n_z + n_heads, dev_sib)
+    per_half = n_units // 4
 
     for i in range(1, n_z):
         red_arrival(red_z, lax.rem(z + i, n_z), 0).wait_recv()
@@ -524,22 +544,26 @@
         device = (lax.div(other, 2), at_ctx(z, lax.rem(other, 2), core))
         red_copy(red_g, head, n_z + i, n_z, device).start()
 
-    @pl.loop(6, n_units)
-    def _(h):
-        backward(h)
-
-    scale = SCALING / acc[0:both, HEAD_DIM : 2 * HEAD_DIM]
-    qg[...] = qg[...] * scale
-    back_copy = remote(
-        qg.at[other_rows], qg_in, back_send.at[0], back_recv.at[0], dev_pair
-    )
-    back_copy.start()
-
-    for i in range(1, n_heads):
-        red_arrival(red_g, lax.rem(head + i, n_heads), n_z).wait_recv()
-    red_c[core] = jnp.sum(red_g[...], axis=0)
-    last = red_copy(red_c, core, n_z + n_heads, n_z + n_heads, dev_sib)
-    last.start()
+    @pl.loop(0, 2 * per_half)
+    def _(i):
+        mine = lax.div(i, per_half)
+        side = 1 - x_lo + mine * (2 * x_lo - 1)
+        backward(
+            4 * (i - mine * per_half), pl.ds(pl.multiple_of(side * rows, 16), rows)
+        )
+
+        @pl.when(i == per_half - 1)
+        def _():
+            qg_out[...] = scaled(other_rows).astype(BF16)
+            back_copy.start()
+
+        @pl.when(i == 2 * per_half - 2)
+        def _():
+            for i in range(1, n_heads):
+                red_arrival(red_g, lax.rem(head + i, n_heads), n_z).wait_recv()
+            red_c[core] = jnp.sum(red_g[...], axis=0)
+            last.start()
+
     for i in range(1, n_z):
         red_copy(red_z, z, i, 0, dev_next).wait_send()
     for i in range(1, n_heads):
@@ -556,9 +580,9 @@
     curvature = jnp.sum(jnp.sum(sums[0:8], axis=0, keepdims=True), axis=1, keepdims=True)
     residual_sq = jnp.sum(jnp.sum(sums[8:16], axis=0, keepdims=True), axis=1, keepdims=True)
     step_size = residual_sq / curvature
-    out_ref[:, own_cols] = dirb[:, own_cols].astype(F32) - step_size * qg[own_rows]
+    out_ref[:, own_cols] = dirb[:, own_cols].astype(F32) - step_size * scaled(own_rows)
     back_copy.wait_recv()
-    out_ref[:, other_cols] = dirb[:, other_cols].astype(F32) - step_size * qg_in[...]
+    out_ref[:, other_cols] = dirb[:, other_cols].astype(F32) - step_size * qg_in[...].astype(F32)
     back_copy.wait_send()
 
 
@@ -592,10 +616,12 @@
             pltpu.VMEM((2, n_group, WINDOW, HEAD_DIM), BF16),
             pltpu.VMEM((both, HEAD_DIM), BF16),
             pltpu.VMEM((both, HEAD_DIM), F32),
-            pltpu.VMEM((rows, HEAD_DIM), F32),
+            pltpu.VMEM((rows, HEAD_DIM), BF16),
+            pltpu.VMEM((rows, HEAD_DIM), BF16),
             pltpu.VMEM((n_z, 16, HEAD_DIM), F32),
             pltpu.VMEM((n_heads, 16, HEAD_DIM), F32),
             pltpu.VMEM((2, 16, HEAD_DIM), F32),
+            pltpu.VMEM((8, HEAD_DIM), F32),
             dma((6,)),
             dma((4,)), dma((4,)),
             dma((2, n_z // 2, 2, 2)), dma((2, n_z // 2, 2, 2)),

time: 82.8 us -> 81.8 us (0.988)
  no operation moved by 1% of the time
where the time goes in v4:
time: 81.8 us; the launch traced here: 81.7 us
  Pallas kernels  80.1 us (98%)
  local copies, waits for them, and re-layouts  1.61 us (2%)
    pallas_call x1, Pallas kernels, body(): pl.pallas_call(functools.partial(kernel, n_group, n_z, rows), out_shape=j...  80.1 us

profile of v4, /device:TPU:1, one launch (start us, length us, event | category | flops | bytes accessed | tf_op | source)
XLA Modules:
  0.0 81.7 jit_solution(8798070583490364925)
XLA Ops:
  0.0 80.1 %gauss_newton_layer.1 = f32[176,256]{1,0:T(8,128)} custom-call(bf16[176,256]{1,0:T(8,128)(2,1)} %q_ref.1, bf16[176,256]{1,0:T(8,128)(2,1)} %k_ref.1, bf16[176,256]{1,0:T(8,128)(2,1)} %v_ref.1, bf16[176,256]{1,0:T(8,128)(2,1)} %d_ref.1, bf16[256,3072]{1,0:T(8,128)(2,1)} %w_ref.1), custom_call_target="tpu_custom_call" | custom-call | tf_op jit(solution)/shard_map/gauss_newton_layer/pallas_call | solution.py:597
  80.1 1.6 %copy.7 = f32[176,256]{1,0:T(8,128)} copy(f32[176,256]{1,0:T(8,128)} %gauss_newton_layer.1) | data formatting | bytes 360448

commit v5 on v4

--- a/solution.py
+++ b/solution.py
@@ -113,11 +113,10 @@
     greet(dev_prev)
     greet(dev_sib)
     greet(dev_pair)
-    for i in range(1, n_group):
-        other = lax.rem(group + i, n_group)
-        greet((other, at_ctx(z, x_lo, core)))
-        greet((other, at_ctx(z, 1 - x_lo, core)))
-    pl.semaphore_wait(barrier, 4 + 2 * (n_group - 1))
+    greet(dev_up)
+    greet(dev_down)
+    greet(dev_across)
+    pl.semaphore_wait(barrier, 7)
 
     swap = [
         remote(
@@ -419,7 +418,7 @@
         )
 
     t_copy(group, 1 - x_lo, 0).start()
-    for i in range(1, n_group):
+    for i in sorted(range(1, n_group), key=lambda i: (0, 2, 3, 2)[i % N_Y], reverse=True):
         other = lax.rem(group + i, n_group)
         t_copy(other, x_lo, 2 * i).start()
         t_copy(other, 1 - x_lo, 2 * i + 1).start()
@@ -467,7 +466,7 @@
     def red_arrival(buf, there, base):
         return remote(buf.at[there], buf.at[there], red_send.at[0], red_recv.at[base + there], dev_pair)
 
-    for i in range(1, n_z):
+    for i in sorted(range(1, n_z), key=lambda i: -min(i, n_z - i)):
         other = lax.rem(z + i, n_z)
         red_copy(red_z, z, i, 0, (group, at_ctx(other, x_lo, core))).start()
 
@@ -539,7 +538,7 @@
     for i in range(1, n_z):
         red_arrival(red_z, lax.rem(z + i, n_z), 0).wait_recv()
     red_g[head] = jnp.sum(red_z[...], axis=0)
-    for i in range(1, n_heads):
+    for i in sorted(range(1, n_heads), key=lambda i: (0, 2, 3, 2)[i // 2 % N_Y], reverse=True):
         other = lax.rem(head + i, n_heads)
         device = (lax.div(other, 2), at_ctx(z, lax.rem(other, 2), core))
         red_copy(red_g, head, n_z + i, n_z, device).start()

time: 81.8 us -> 80.8 us (0.988)
  Pallas kernels: 80.1 us -> 79 us
    pallas_call x1, Pallas kernels: 80.1 us -> 79 us  [body(): pl.pallas_call(functools.partial(kernel, n_group, n_z, rows), out_shape=j...]
where the time goes in v5:
time: 80.8 us; the launch traced here: 80.6 us
  Pallas kernels  79 us (98%)
  local copies, waits for them, and re-layouts  1.61 us (2%)
    pallas_call x1, Pallas kernels, body(): pl.pallas_call(functools.partial(kernel, n_group, n_z, rows), out_shape=j...  79 us

profile of v5, /device:TPU:1, one launch (start us, length us, event | category | flops | bytes accessed | tf_op | source)
XLA Modules:
  0.0 80.6 jit_solution(2832508567509126267)
XLA Ops:
  0.0 79.0 %gauss_newton_layer.1 = f32[176,256]{1,0:T(8,128)} custom-call(bf16[176,256]{1,0:T(8,128)(2,1)} %q_ref.1, bf16[176,256]{1,0:T(8,128)(2,1)} %k_ref.1, bf16[176,256]{1,0:T(8,128)(2,1)} %v_ref.1, bf16[176,256]{1,0:T(8,128)(2,1)} %d_ref.1, bf16[256,3072]{1,0:T(8,128)(2,1)} %w_ref.1), custom_call_target="tpu_custom_call" | custom-call | tf_op jit(solution)/shard_map/gauss_newton_layer/pallas_call | solution.py:596
  79.0 1.6 %copy.7 = f32[176,256]{1,0:T(8,128)} copy(f32[176,256]{1,0:T(8,128)} %gauss_newton_layer.1) | data formatting | bytes 360448

commit v6 on v5

--- a/solution.py
+++ b/solution.py
@@ -166,13 +166,18 @@
         place = chunk(p, core_, part_of(o))
         return remote(place, place, sib_send.at[p, o], sib_recv.at[p, o], dev_sib)
 
+    for f in range(2):
+        for way in range(2):
+            remote(
+                (k_ref, v_ref)[f].at[:, own_cols],
+                kv.at[chunk_rows(1 + way, core, x_lo), f * HEAD_DIM : (f + 1) * HEAD_DIM],
+                ring_send.at[way, 0, 0, f], ring_recv.at[way, 0, 0, f],
+                dev_prev if way else dev_next,
+            ).start()
+    swap[2].start()
+    swap[3].start()
     local[0].wait()
     local[1].wait()
-    for f in range(2):
-        ring(0, 1, 0, f, 0, 1).start()
-        ring(1, 1, 0, f, 0, 2).start()
-    swap[2].start()
-    swap[3].start()
     sibling(0, 0, core).start()
 
     def w_copy(n, src, dst, device):

time: 80.8 us -> 80.8 us (level)
  no operation moved by 1% of the time
where the time goes in v6:
time: 80.8 us; the launch traced here: 80.6 us
  Pallas kernels  79 us (98%)
  local copies, waits for them, and re-layouts  1.61 us (2%)
    pallas_call x1, Pallas kernels, body(): pl.pallas_call(functools.partial(kernel, n_group, n_z, rows), out_shape=j...  79 us

profile of v6, /device:TPU:1, one launch (start us, length us, event | category | flops | bytes accessed | tf_op | source)
XLA Modules:
  0.0 80.6 jit_solution(7193521443253482908)
XLA Ops:
  0.0 79.0 %gauss_newton_layer.1 = f32[176,256]{1,0:T(8,128)} custom-call(bf16[176,256]{1,0:T(8,128)(2,1)} %q_ref.1, bf16[176,256]{1,0:T(8,128)(2,1)} %k_ref.1, bf16[176,256]{1,0:T(8,128)(2,1)} %v_ref.1, bf16[176,256]{1,0:T(8,128)(2,1)} %d_ref.1, bf16[256,3072]{1,0:T(8,128)(2,1)} %w_ref.1), custom_call_target="tpu_custom_call" | custom-call | tf_op jit(solution)/shard_map/gauss_newton_layer/pallas_call | solution.py:601
  79.0 1.6 %copy.7 = f32[176,256]{1,0:T(8,128)} copy(f32[176,256]{1,0:T(8,128)} %gauss_newton_layer.1) | data formatting | bytes 360448
